TPU v7x, 256 devices: a whole 4x4x8 slice. The times are simulated.
256 devices in a mesh: ha: 16 (over z, y_lo), ta: 8 (over y_hi, x), col: 2 (over core).
Axes of the slice: x: 4, y: 4 (y_hi: 2, y_lo: 2; y = y_hi * 2 + y_lo), z: 8, core: 2. Of those that a mesh axis runs over, the one named last changes fastest.
Arguments:
- tokens: bfloat16 [64, 448, 28, 128], P(('col', 'ta'), 'ha'), parts along dimension 0, may hold values from -6 to 6
- regions_one: int32 [64, 448, 28], P(('col', 'ta'), 'ha'), parts along dimension 0, may hold values from 0 to 2
- regions_three: int32 [64, 112, 7], P(('col', 'ta'), 'ha'), parts along dimension 0, may hold values from 0 to 2
- gain_one: float32 [128], replicated, may hold values from 0.25 to 1.75
- projection_one: bfloat16 [128, 384], replicated, may hold values from -0.5 to 0.5
- outward_one: bfloat16 [128, 128], replicated, may hold values from -0.5 to 0.5
- table_one: float32 [1183, 4], replicated, may hold values from -4 to 303
- merge_gain_one: float32 [512], replicated, may hold values from 0.25 to 1.75
- merge_weight_one: bfloat16 [512, 256], replicated, may hold values from -0.25 to 0.25
- merge_gain_two: float32 [1024], replicated, may hold values from 0.25 to 1.75
- merge_weight_two: bfloat16 [1024, 512], replicated, may hold values from -0.1875 to 0.1875
- gain_three: float32 [512], replicated, may hold values from 0.25 to 1.75
- projection_three: bfloat16 [512, 1536], replicated, may hold values from -0.25 to 0.25
- outward_three: bfloat16 [512, 512], replicated, may hold values from -0.25 to 0.25
- table_three: float32 [1183, 16], replicated, may hold values from -4 to 303
- cotangent: bfloat16 [64, 112, 7, 512], P(('col', 'ta'), 'ha'), parts along dimension 0, may hold values from -6 to 6
Outputs:
- section_three: bfloat16 [64, 112, 7, 512], P(('col', 'ta'), 'ha'), parts along dimension 0
- grad_tokens: bfloat16 [64, 448, 28, 128], P(('col', 'ta'), 'ha'), parts along dimension 0
There are 2 independent parts, one for each index of `col`. A program takes and returns all parts, laid end to end along the dimension named above; an argument that names none is the same for every part. Nothing has to cross between parts.
Inputs may be any that keep to these rules, and one draw needn't show every extreme that they name: `regions_one`: region ids are free for each position. `regions_three`: region ids are free for each position.
All inputs are finite; a program needn't handle non-finite values.
Results may differ from a plain program's by a relative error of at most 0.03.
Values may be sent and summed in bfloat16 or wider, within the bound.
A program may use at most 192 MiB of HBM per device.

v0:
```python
import functools
import math

import jax
import jax.numpy as jnp
from jax import lax
from jax.experimental import pallas as pl
from jax.experimental.pallas import tpu as pltpu
from jax.sharding import PartitionSpec as P

F32 = jnp.float32
BF16 = jnp.bfloat16

C1 = 128
C3 = 512
HEADS1 = 4
HEADS3 = 16
HEAD = 32
EPSILON = 1e-05

GROUPS = 28
ROWS = 224
LANES = 256
WINDOWS = 20
FIRST = 10
OWN = 28 - FIRST
NEXT = 35 - OWN

LOG2E = math.log2(math.e)
LN2 = math.log(2.0)
SCALE = HEAD**-0.5
LEFT_OUT = 1e30

TABLE_LANES = 1408
DEPTH = 768
ALL_HEADS = HEADS1 + HEADS3


def dot(a, b):
    return jnp.dot(a, b, preferred_element_type=F32)


def dot_t(a, b):
    return lax.dot_general(a, b, (((1,), (1,)), ((), ())), preferred_element_type=F32)


def normalised(x):
    centred = x - jnp.mean(x, -1, keepdims=True)
    inverse = lax.rsqrt(jnp.mean(centred * centred, -1, keepdims=True) + EPSILON)
    return centred * inverse, inverse


def norm_pull(grad, hat, inverse, gain):
    scaled = grad * gain
    mean = jnp.mean(scaled, -1, keepdims=True)
    along = jnp.mean(scaled * hat, -1, keepdims=True)
    return inverse * (scaled - mean - hat * along)


def rounded(x):
    return x.astype(BF16).astype(F32)


def head_mask(head):
    lane = lax.broadcasted_iota(jnp.int32, (1, C1), 1)
    return jnp.where((lane >= HEAD * head) & (lane < HEAD * (head + 1)), 1.0, 0.0).astype(BF16)


def padded(x):
    return jnp.concatenate([x, jnp.zeros((LANES - ROWS, x.shape[1]), x.dtype)], 0)


def attend(q, k, values_t, hot, bias_ref, bias_at, probs_ref, at):
    k_wide = jnp.concatenate([k, hot], 1)
    apart = padded((hot - 1.0) * jnp.array(LEFT_OUT, BF16))
    q = padded(q)
    out = []
    for head in range(4):
        q_wide = jnp.concatenate([q * head_mask(head), apart], 1)
        scores = dot_t(k_wide, q_wide)
        for half in range(2):
            lanes = slice(128 * half, 128 * half + 128)
            place = slice(LANES * head + 128 * half, LANES * head + 128 * half + 128)
            part = scores[:, lanes] + bias_ref[bias_at, :, place]
            raised = jnp.exp2(part - jnp.max(part, 0, keepdims=True))
            share = 1.0 / jnp.sum(raised, 0, keepdims=True)
            probs_ref[at, :, place] = (raised * share).astype(BF16)
        probs = probs_ref[at, :, LANES * head : LANES * head + LANES]
        out.append(dot(values_t[HEAD * head : HEAD * head + HEAD], probs))
    return jnp.concatenate(out, 0)


def attend_pull(d_out, d_out_t, out_t, q, keys_t, values, probs_ref, at):
    product = d_out_t * out_t
    q = padded(q)
    d_values = jnp.zeros((ROWS, C1), F32)
    d_keys = jnp.zeros((ROWS, C1), F32)
    d_queries = []
    for head in range(4):
        rows = slice(HEAD * head, HEAD * head + HEAD)
        mask = head_mask(head)
        d_head = d_out * mask
        probs = probs_ref[at, :, LANES * head : LANES * head + LANES]
        d_probs = dot_t(values, d_head)
        delta = jnp.sum(product[rows], 0, keepdims=True)
        d_scores = (probs.astype(F32) * (d_probs - delta)).astype(BF16)
        d_values += dot(probs, d_head)
        d_keys += dot(d_scores, q * mask)
        d_queries.append(dot(keys_t[rows], d_scores))
    d_q = jnp.transpose(jnp.concatenate(d_queries, 0) * SCALE)[:ROWS]
    return jnp.concatenate([d_q.astype(BF16), (d_keys * LN2).astype(BF16), d_values.astype(BF16)], 1)


def bias_kernel(table_ref, one_ref, three_ref, wide_ref):
    for head in range(ALL_HEADS):
        row = jnp.broadcast_to(table_ref[head : head + 1, :] * LOG2E, (8, TABLE_LANES))
        for frame in range(4):
            start = 14 + 169 * (3 - frame)
            moved = pltpu.roll(row, TABLE_LANES - start, 1, stride=1, stride_axis=0)
            first = (frame * ALL_HEADS + head) * 8
            wide_ref[first : first + 8, :] = moved[:, :DEPTH]
    wide = wide_ref[...]
    high = wide.astype(BF16)
    low = (wide - high.astype(F32)).astype(BF16)
    lane = lax.broadcasted_iota(jnp.int32, (DEPTH, LANES), 1)
    depth = lax.broadcasted_iota(jnp.int32, (DEPTH, LANES), 0)
    group = lane >> 3
    column = lane & 7
    frame = (group * 9363) >> 16
    line = group - 7 * frame
    offset = 169 * frame + 13 * line + column
    valid = (column < 7) & (lane < ROWS)
    for key_line in range(7):
        chosen = valid & (depth == offset + 13 * (6 - key_line))
        chosen = jnp.where(chosen, 1.0, 0.0).astype(BF16)
        picked = dot(high, chosen) + dot(low, chosen)
        for key_frame in range(4):
            to = slice(key_frame * 56 + key_line * 8, key_frame * 56 + key_line * 8 + 8)
            for head in range(ALL_HEADS):
                first = (key_frame * ALL_HEADS + head) * 8
                block = picked[first : first + 8]
                if head < HEADS1:
                    one_ref[0, to, head * LANES : (head + 1) * LANES] = block
                else:
                    group_at, place = divmod(head - HEADS1, 4)
                    three_ref[group_at, to, place * LANES : (place + 1) * LANES] = block


def expand_tables(tables):
    return pl.pallas_call(
        bias_kernel,
        out_shape=(
            jax.ShapeDtypeStruct((1, ROWS, 4 * LANES), F32),
            jax.ShapeDtypeStruct((4, ROWS, 4 * LANES), F32),
        ),
        in_specs=[pl.BlockSpec(memory_space=pltpu.VMEM)],
        out_specs=(pl.BlockSpec(memory_space=pltpu.VMEM), pl.BlockSpec(memory_space=pltpu.VMEM)),
        scratch_shapes=[pltpu.VMEM((4 * ALL_HEADS * 8, DEPTH), F32)],
        compiler_params=pltpu.CompilerParams(vmem_limit_bytes=48 * 2**20),
        cost_estimate=pl.CostEstimate(flops=4 * 10**9, bytes_accessed=6 * 10**6, transcendentals=0),
        name="expand_tables",
    )(tables)


def main_kernel(
    tokens,
    tokens_ta,
    tokens_ha,
    tokens_both,
    cot,
    cot_ta,
    cot_ha,
    cot_both,
    hot_one,
    hot_three,
    bias_one,
    bias_three,
    gain_one,
    projection_one,
    kv_one_t,
    outward_one,
    merge_gain_one,
    merge_weight_one,
    merge_gain_two,
    merge_weight_two,
    gain_three,
    projection_three,
    kv_three_t,
    outward_three,
    section_out,
    grad_out,
    grid,
    folded,
    windows,
    mixed,
    probs_one,
    q_one,
    kt_one,
    v_one,
    out_t_one,
    grouped,
    inverse_one,
    merged,
    probs_three,
    q_three,
    k_three,
    v_three,
    kt_three,
    vt_three,
    out_t_three,
    out_three,
    d_out_three,
    d_out_t_three,
    d_packed_three,
    cot_wide,
):
    def place_row(frame, row, values):
        values = values.astype(F32)
        grid[frame, row, 0:28, :] = values
        grid[frame, row, 28:36, :] = values[0:8]

    def own_rows(row, _):
        for frame in range(2):
            place_row(frame, row, tokens[2 + frame, FIRST + row])
            place_row(2 + frame, row, tokens_ta[frame, row])
        return 0

    def next_rows(row, _):
        for frame in range(2):
            place_row(frame, OWN + row, tokens_ha[frame, row])
            place_row(2 + frame, OWN + row, tokens_both[frame, row])
        return 0

    lax.fori_loop(0, OWN, own_rows, 0)
    lax.fori_loop(0, NEXT, next_rows, 0)

    def cut(k, _):
        for m in range(4):
            for frame in range(4):
                for row in range(7):
                    group = (frame * 7 + row) * 8
                    windows[4 * k + m, group : group + 8, :] = grid[frame, 7 * k + row, 3 + 7 * m : 11 + 7 * m, :]
        return 0

    lax.fori_loop(0, 5, cut, 0)

    def forward_one(at, _):
        x = windows[at]
        hat, _unused = normalised(x)
        normed = (hat * gain_one[...]).astype(BF16)
        packed = dot(normed, projection_one[...])
        packed_t = dot_t(kv_one_t[...], normed).astype(BF16)
        q = (packed[:, :C1] * (SCALE * LOG2E)).astype(BF16)
        v_one[at] = packed[:, 2 * C1 :].astype(BF16)
        q_one[at] = q
        kt_one[at] = packed_t[:C1]
        out_t = attend(q, packed[:, C1 : 2 * C1].astype(BF16), packed_t[C1:], hot_one[at], bias_one, 0, probs_one, at)
        out_t_one[at] = out_t.astype(BF16)
        out = jnp.transpose(out_t)[:ROWS].astype(BF16)
        mixed[at] = rounded(x + rounded(dot(out, outward_one[...])))
        return 0

    lax.fori_loop(0, WINDOWS, forward_one, 0)

    def uncut(k, _):
        for frame in range(4):
            for row in range(7):
                group = (frame * 7 + row) * 8
                folded[frame, 7 * k + row, 28:35, :] = mixed[4 * k, group : group + 7, :]
                second = mixed[4 * k + 1, group : group + 7, :]
                folded[frame, 7 * k + row, 7:14, :] = second
                folded[frame, 7 * k + row, 35:42, :] = second
                folded[frame, 7 * k + row, 14:21, :] = mixed[4 * k + 2, group : group + 7, :]
                folded[frame, 7 * k + row, 21:28, :] = mixed[4 * k + 3, group : group + 7, :]
        return 0

    lax.fori_loop(0, 5, uncut, 0)

    def gather_blocks(frame, _):
        for row in range(7):
            group = (frame * 7 + row) * 8
            for a in range(2):
                for b in range(2):
                    for p in range(2):
                        for q in range(2):
                            block = 2 * q + p
                            grouped[2 * b + a, pl.ds(pl.multiple_of(group, 8), 8), 128 * block : 128 * block + 128] = folded[
                                frame, 2 + 4 * row + 2 * a + p, pl.ds(9 + 2 * b + q, 8, stride=4), :
                            ]
        return 0

    lax.fori_loop(0, 4, gather_blocks, 0)

    for place in range(4):
        hat, inverse = normalised(grouped[place])
        grouped[place] = hat
        inverse_one[place] = jnp.broadcast_to(inverse, (ROWS, 128))
        merged[:, 256 * place : 256 * place + 256] = rounded(
            dot((hat * merge_gain_one[...]).astype(BF16), merge_weight_one[...])
        )
    hat_two, inverse_two = normalised(merged[...])
    merged[...] = hat_two
    merged_two = rounded(dot((hat_two * merge_gain_two[...]).astype(BF16), merge_weight_two[...]))
    hat_three, inverse_three = normalised(merged_two)
    normed_three = (hat_three * gain_three[...]).astype(BF16)

    packed = dot(normed_three, projection_three[...])
    packed_t = dot_t(kv_three_t[...], normed_three).astype(BF16)
    for g in range(4):
        q_three[g] = (packed[:, C1 * g : C1 * g + C1] * (SCALE * LOG2E)).astype(BF16)
        k_three[g] = packed[:, C3 + C1 * g : C3 + C1 * g + C1].astype(BF16)
        v_three[g] = packed[:, 2 * C3 + C1 * g : 2 * C3 + C1 * g + C1].astype(BF16)
        kt_three[g] = packed_t[C1 * g : C1 * g + C1]
        vt_three[g] = packed_t[C3 + C1 * g : C3 + C1 * g + C1]

    def forward_three(g, _):
        out_t = attend(q_three[g], k_three[g], vt_three[g], hot_three[...], bias_three, g, probs_three, g)
        out_t_three[g] = out_t.astype(BF16)
        out_three[g] = jnp.transpose(out_t)[:ROWS].astype(BF16)
        return 0

    lax.fori_loop(0, 4, forward_three, 0)
    out = jnp.concatenate([out_three[g] for g in range(4)], 1)
    section = merged_two + rounded(dot(out, outward_three[...]))
    section_out[...] = section.astype(BF16)

    for frame in range(4):
        for row in range(7):
            if row < 4:
                source = cot[2 + frame, 3 + row] if frame < 2 else cot_ta[frame - 2, row]
            else:
                source = cot_ha[frame, row - 4] if frame < 2 else cot_both[frame - 2, row - 4]
            source = source.astype(F32)
            group = (frame * 7 + row) * 8
            cot_wide[group : group + 4, :] = source[3:7]
            cot_wide[group + 4 : group + 7, :] = source[0:3]
            cot_wide[group + 7 : group + 8, :] = jnp.zeros((1, C3), F32)
    d_section = cot_wide[...]
    d_mixed = padded(d_section.astype(BF16))
    d_out = dot_t(d_mixed, outward_three[...]).astype(BF16)
    d_out_t = dot_t(outward_three[...], d_mixed)
    for g in range(4):
        d_out_three[g] = d_out[:, C1 * g : C1 * g + C1]
        d_out_t_three[g] = d_out_t[C1 * g : C1 * g + C1]

    def backward_three(g, _):
        d_packed_three[g] = attend_pull(
            d_out_three[g],
            d_out_t_three[g],
            out_t_three[g].astype(F32),
            q_three[g],
            kt_three[g],
            v_three[g],
            probs_three,
            g,
        )
        return 0

    lax.fori_loop(0, 4, backward_three, 0)
    d_packed = jnp.concatenate(
        [d_packed_three[g, :, C1 * part : C1 * part + C1] for part in range(3) for g in range(4)], 1
    )
    d_normed = rounded(dot_t(d_packed, projection_three[...]))
    d_merged_two = d_section + rounded(norm_pull(d_normed, hat_three, inverse_three, gain_three[...]))
    d_grouped_two = dot_t(d_merged_two.astype(BF16), merge_weight_two[...])
    d_merged_one = norm_pull(d_grouped_two, merged[...], inverse_two, merge_gain_two[...]).astype(BF16)
    for place in range(4):
        d_grouped = dot_t(d_merged_one[:, 256 * place : 256 * place + 256], merge_weight_one[...])
        grouped[place] = norm_pull(d_grouped, grouped[place], inverse_one[place][:, :1], merge_gain_one[...])

    for frame in range(4):
        for row in (0, 1, 30, 31, 32, 33, 34):
            folded[frame, row] = jnp.zeros((48, C1), F32)

    def scatter_blocks(frame, _):
        for row in range(7):
            group = (frame * 7 + row) * 8
            for a in range(2):
                for b in range(2):
                    for p in range(2):
                        for q in range(2):
                            block = 2 * q + p
                            folded[frame, 2 + 4 * row + 2 * a + p, pl.ds(9 + 2 * b + q, 8, stride=4), :] = grouped[
                                2 * b + a, pl.ds(pl.multiple_of(group, 8), 8), 128 * block : 128 * block + 128
                            ]
        return 0

    lax.fori_loop(0, 4, scatter_blocks, 0)

    def cut_back(k, _):
        for frame in range(4):
            for row in range(7):
                group = (frame * 7 + row) * 8
                folded[frame, 7 * k + row, 7:9, :] = folded[frame, 7 * k + row, 35:37, :]
                mixed[4 * k, group : group + 8, :] = folded[frame, 7 * k + row, 28:36, :]
                for m in range(1, 4):
                    mixed[4 * k + m, group : group + 8, :] = folded[frame, 7 * k + row, 7 * m : 7 * m + 8, :]
        return 0

    lax.fori_loop(0, 5, cut_back, 0)

    def backward_one(at, _):
        hat, inverse = normalised(windows[at])
        d_residual = rounded(mixed[at])
        d_mixed = padded(d_residual.astype(BF16))
        d_out = dot_t(d_mixed, outward_one[...]).astype(BF16)
        d_out_t = dot_t(outward_one[...], d_mixed)
        d_packed = attend_pull(
            d_out, d_out_t, out_t_one[at].astype(F32), q_one[at], kt_one[at], v_one[at], probs_one, at
        )
        d_normed = rounded(dot_t(d_packed, projection_one[...]))
        mixed[at] = d_residual + norm_pull(d_normed, hat, inverse, gain_one[...])
        return 0

    lax.fori_loop(0, WINDOWS, backward_one, 0)

    def place_back(k, _):
        for frame in range(4):
            for row in range(7):
                group = (frame * 7 + row) * 8
                for m in range(3):
                    grid[frame, 7 * k + row, 3 + 7 * m : 10 + 7 * m, :] = mixed[4 * k + m, group : group + 7, :]
                grid[frame, 7 * k + row, 24:28, :] = mixed[4 * k + 3, group : group + 4, :]
                grid[frame, 7 * k + row, 0:3, :] = mixed[4 * k + 3, group + 4 : group + 7, :]
                grad_out[frame, 7 * k + row] = grid[frame, 7 * k + row, 0:28, :].astype(BF16)
        return 0

    lax.fori_loop(0, 5, place_back, 0)


def main_call(*operands):
    vmem = pl.BlockSpec(memory_space=pltpu.VMEM)
    return pl.pallas_call(
        main_kernel,
        out_shape=(
            jax.ShapeDtypeStruct((ROWS, C3), BF16),
            jax.ShapeDtypeStruct((4, 35, 28, C1), BF16),
        ),
        in_specs=[vmem] * len(operands),
        out_specs=(vmem, vmem),
        scratch_shapes=[
            pltpu.VMEM((4, 35, 40, C1), F32),
            pltpu.VMEM((4, 35, 48, C1), F32),
            pltpu.VMEM((WINDOWS, ROWS, C1), F32),
            pltpu.VMEM((WINDOWS, ROWS, C1), F32),
            pltpu.VMEM((WINDOWS, ROWS, 4 * LANES), BF16),
            pltpu.VMEM((WINDOWS, ROWS, C1), BF16),
            pltpu.VMEM((WINDOWS, C1, ROWS), BF16),
            pltpu.VMEM((WINDOWS, ROWS, C1), BF16),
            pltpu.VMEM((WINDOWS, C1, LANES), BF16),
            pltpu.VMEM((4, ROWS, 512), F32),
            pltpu.VMEM((4, ROWS, 128), F32),
            pltpu.VMEM((ROWS, 1024), F32),
            pltpu.VMEM((4, ROWS, 4 * LANES), BF16),
            pltpu.VMEM((4, ROWS, C1), BF16),
            pltpu.VMEM((4, ROWS, C1), BF16),
            pltpu.VMEM((4, ROWS, C1), BF16),
            pltpu.VMEM((4, C1, ROWS), BF16),
            pltpu.VMEM((4, C1, ROWS), BF16),
            pltpu.VMEM((4, C1, LANES), BF16),
            pltpu.VMEM((4, ROWS, C1), BF16),
            pltpu.VMEM((4, LANES, C1), BF16),
            pltpu.VMEM((4, C1, LANES), F32),
            pltpu.VMEM((4, ROWS, 3 * C1), BF16),
            pltpu.VMEM((ROWS, C3), F32),
        ],
        compiler_params=pltpu.CompilerParams(vmem_limit_bytes=60 * 2**20),
        cost_estimate=pl.CostEstimate(flops=3 * 10**10, bytes_accessed=2 * 10**7, transcendentals=4 * 10**6),
        name="sections",
    )(*operands)


def send(values, ha_by, ta_by):
    ha_count, ta_count = lax.axis_size("ha"), lax.axis_size("ta")
    pairs = []
    for h in range(ha_count):
        for t in range(ta_count):
            to = ((h + ha_by) % ha_count) * ta_count + (t + ta_by) % ta_count
            pairs.append((h * ta_count + t, to))
    return lax.ppermute(values, ("ha", "ta"), pairs)


def one_hot_regions(ids):
    ids = jnp.pad(ids, ((0, 0), (0, 0), (0, 1)), constant_values=3)
    ids = ids.reshape(-1, ROWS)
    return (ids[:, :, None] == jnp.arange(128, dtype=jnp.int32)).astype(BF16)


def per_device(
    tokens,
    regions_one,
    regions_three,
    gain_one,
    projection_one,
    outward_one,
    table_one,
    merge_gain_one,
    merge_weight_one,
    merge_gain_two,
    merge_weight_two,
    gain_three,
    projection_three,
    outward_three,
    table_three,
    cotangent,
):
    tokens_ta = send(tokens[:2, FIRST:], 0, -1)
    tokens_ha = send(tokens[2:, :NEXT], -1, 0)
    tokens_both = send(tokens[:2, :NEXT], -1, -1)
    cot_ta = send(cotangent[:2, 3:], 0, -1)
    cot_ha = send(cotangent[2:, :3], -1, 0)
    cot_both = send(cotangent[:2, :3], -1, -1)
    regions_next = send(regions_one[:, :14], -1, 0)

    tables = jnp.concatenate([table_one, table_three], 1).T
    tables = jnp.pad(tables, ((0, 0), (8, TABLE_LANES - 8 - tables.shape[1])))
    bias_one, bias_three = expand_tables(tables)

    ids = jnp.concatenate([regions_one[:, 7:], regions_next], 1)
    ids = ids.reshape(4, 5, 7, 4, 7).transpose(1, 3, 0, 2, 4).reshape(WINDOWS, GROUPS, 7)
    hot_one = one_hot_regions(ids)
    hot_three = one_hot_regions(regions_three.reshape(1, GROUPS, 7))[0]

    section, grad = main_call(
        tokens,
        tokens_ta,
        tokens_ha,
        tokens_both,
        cotangent,
        cot_ta,
        cot_ha,
        cot_both,
        hot_one,
        hot_three,
        bias_one,
        bias_three,
        gain_one.reshape(1, -1),
        projection_one,
        projection_one[:, C1:].T,
        outward_one,
        merge_gain_one.reshape(1, -1),
        merge_weight_one,
        merge_gain_two.reshape(1, -1),
        merge_weight_two,
        gain_three.reshape(1, -1),
        projection_three,
        projection_three[:, C3:].T,
        outward_three,
    )

    section = section.reshape(4, 7, 8, C3)
    section = jnp.concatenate([section[:, :, 4:7], section[:, :, :4]], 2)
    from_ta = send(section[2:, :4], 0, 1)
    from_ha = send(section[:2, 4:], 1, 0)
    from_both = send(section[2:, 4:], 1, 1)
    finished = jnp.concatenate(
        [jnp.concatenate([from_both, from_ta], 1), jnp.concatenate([from_ha, section[:2, :4]], 1)], 0
    )

    grad_ta = send(grad[2:, :OWN], 0, 1)
    grad_ha = send(grad[:2, OWN:], 1, 0)
    grad_both = send(grad[2:, OWN:], 1, 1)

    def joined(behind, own):
        shared = behind[:, FIRST:].astype(F32) + own[:, : NEXT - FIRST].astype(F32)
        return jnp.concatenate([behind[:, :FIRST], shared.astype(BF16), own[:, NEXT - FIRST :]], 1)

    grad_total = jnp.concatenate([joined(grad_both, grad_ta), joined(grad_ha, grad[:2, :OWN])], 0)
    return (finished, grad_total)


def solution(mesh):
    wide = P(("col", "ta"), "ha", None, None)
    flat = P(("col", "ta"), "ha", None)
    in_specs = (wide, flat, flat) + (P(),) * 12 + (wide,)
    return jax.shard_map(per_device, mesh=mesh, in_specs=in_specs, out_specs=(wide, wide), check_vma=False)
```

profile of v0, /device:TPU:1, one launch (start us, length us, event | category | flops | bytes accessed | tf_op | source)
XLA Modules:
  0.0 157.9 jit_solution(15177567638832278037)
XLA Ops:
  0.6 0.8 slice.91
  1.5 7.4 %collective-permute-start.6 = (s32[4,14,28]{2,0,1:T(4,128)S(1)}, s32[4,14,28]{2,0,1:T(4,128)S(1)}, u32[]{:S(2)}, u32[]{:S(2)}) collective-permute-start(s32[4,14,28]{2,0,1:T(4,128)S(1)} %slice.91), channel_id=1, source_target_pairs={{0,240},{2,242},{4,244},{6,246},{8,248},{10,250},{12,252},{14,254}... | collective-permute-start | bytes 18824 | tf_op jit(solution)/shard_map/ppermute | solution.py:480
  8.9 1.0 copy.45.cot
  9.9 4.9 %collective-permute-start.3 = (bf16[2,4,7,512]{3,2,1,0:T(8,128)(2,1)S(1)}, bf16[2,4,7,512]{3,2,1,0:T(8,128)(2,1)S(1)}, u32[]{:S(2)}, u32[]{:S(2)}) collective-permute-start(bf16[2,4,7,512]{3,2,1,0:T(8,128)(2,1)S(1)} %slice.114), channel_id=1, source_target_pairs={{0,14},{2,0},{4,2},{6,4},{8,6},{10,8},{12,10},{14,12},{16,30},{18,... | collective-permute-start | bytes 172040 | tf_op jit(solution)/shard_map/ppermute | solution.py:480
  14.8 0.1 collective-permute-start.5
  14.9 0.7 collective-permute-start.4
  15.5 0.1 copy.44.tokens
  15.7 0.0 copy-start.8
  15.7 0.0 copy-start.6
  15.8 1.8 %collective-permute-start = (bf16[2,18,28,128]{3,2,1,0:T(8,128)(2,1)S(1)}, bf16[2,18,28,128]{3,2,1,0:T(8,128)(2,1)}, u32[]{:S(2)}, u32[]{:S(2)}) collective-permute-start(bf16[2,18,28,128]{3,2,1,0:T(8,128)(2,1)S(1)} %slice.111), channel_id=1, source_target_pairs={{0,14},{2,0},{4,2},{6,4},{8,6},{10,8},{12,10},{14,12},{16,30},{18,... | collective-permute-start | bytes 774152 | tf_op jit(solution)/shard_map/ppermute | solution.py:480
  17.7 0.1 eq.37
  17.8 0.1 pad.14.table_ref
  17.9 0.0 slice-start.1
  17.9 3.9 %expand_tables.1 = (f32[1,224,1024]{2,1,0:T(8,128)S(1)}, f32[4,224,1024]{2,1,0:T(8,128)S(1)}) custom-call(f32[20,1408]{1,0:T(8,128)S(1)} %pad.14.table_ref), custom_call_target="tpu_custom_call" | custom-call | flops 4000000000 | bytes 6000000 | tf_op jit(solution)/shard_map/expand_tables/pallas_call | solution.py:150
  21.9 1.8 %copy-done = f32[4,224,1024]{2,1,0:T(8,128)} copy-done((f32[4,224,1024]{2,1,0:T(8,128)}, f32[4,224,1024]{2,1,0:T(8,128)S(1)}, u32[]{:S(2)}) %copy-start) | copy-done | bytes 3670040
  23.7 1.0 copy-done.1
  24.7 0.7 fusion.1.hot_three
  25.4 0.7 copy.49
  26.1 0.5 slice-done
  26.6 1.3 copy.50
  28.0 0.2 reshape.42
  28.2 0.6 copy.37
  28.8 0.2 reshape.43
  29.0 0.1 copy.53
  29.2 0.1 copy.39
  29.3 1.0 collective-permute-start.1
  30.3 1.6 fusion.hot_one
  31.9 0.0 copy-start.11
  31.9 3.1 %collective-permute-done.2.tokens_both = bf16[2,17,28,128]{3,2,1,0:T(8,128)(2,1)S(1)} collective-permute-done((bf16[2,17,28,128]{3,2,1,0:T(8,128)(2,1)S(1)}, bf16[2,17,28,128]{3,2,1,0:T(8,128)(2,1)S(1)}, u32[]{:S(2)}, u32[]{:S(2)}) %collective-permute-start.2) | collective-permute-done | bytes 243744 | tf_op jit(solution)/shard_map/ppermute | solution.py:480
  35.0 8.4 %collective-permute-done.1.tokens_ha = bf16[2,17,28,128]{3,2,1,0:T(8,128)(2,1)S(1)} collective-permute-done((bf16[2,17,28,128]{3,2,1,0:T(8,128)(2,1)S(1)}, bf16[2,17,28,128]{3,2,1,0:T(8,128)(2,1)S(1)}, u32[]{:S(2)}, u32[]{:S(2)}) %collective-permute-start.1) | collective-permute-done | bytes 243744 | tf_op jit(solution)/shard_map/ppermute | solution.py:480
  43.4 0.7 copy-done.10
  44.1 78.1 %sections.1 = (bf16[224,512]{1,0:T(8,128)(2,1)}, bf16[4,35,28,128]{3,2,1,0:T(8,128)(2,1)}) custom-call(bf16[4,28,28,128]{3,2,1,0:T(8,128)(2,1)} %copy-done.2, bf16[2,18,28,128]{3,2,1,0:T(8,128)(2,1)} %collective-permute-done.tokens_ta, bf16[2,17,28,128]{3,2,1,0:T(8,128)(2,1)} %copy-done.10, bf16[2,17,28,128]{3,2,1,0:T(8,128)(2,1)} %copy-done.9, ...), custom_call_target="tpu_custom_call" | custom-call | flops 30000001024 | bytes 20000000 | tf_op jit(solution)/shard_map/sections/pallas_call | solution.py:433
  122.2 1.0 slice.117
  123.3 1.1 slice.118
  124.4 0.1 copy_dynamic-update-slice_fusion
  124.4 0.1 fusion.6
  124.5 1.4 collective-permute-start.8
  125.9 1.1 fusion.2
  127.0 0.1 collective-permute-start.10
  127.1 2.4 %collective-permute-start.12 = (bf16[2,17,28,128]{3,2,1,0:T(8,128)(2,1)S(1)}, bf16[2,17,28,128]{3,2,1,0:T(8,128)(2,1)S(1)}, u32[]{:S(2)}, u32[]{:S(2)}) collective-permute-start(bf16[2,17,28,128]{3,2,1,0:T(8,128)(2,1)S(1)} %get-tuple-element.15), channel_id=1, source_target_pairs={{0,16},{2,18},{4,20},{6,22},{8,24},{10,26},{12,28},{14,30},{16,32}... | collective-permute-start | bytes 731144 | tf_op jit(solution)/shard_map/ppermute | solution.py:480
  129.5 0.1 fusion.5
  129.6 0.2 collective-permute-start.7
  129.8 0.0 collective-permute-start.9
  129.8 16.8 %collective-permute-done.7 = bf16[2,3,7,512]{3,0,2,1:T(2,128)(2,1)S(1)} collective-permute-done((bf16[2,3,7,512]{3,0,2,1:T(2,128)(2,1)S(1)}, bf16[2,3,7,512]{3,0,2,1:T(2,128)(2,1)S(1)}, u32[]{:S(2)}, u32[]{:S(2)}) %collective-permute-start.7) | collective-permute-done | bytes 43040 | tf_op jit(solution)/shard_map/ppermute | solution.py:480
  146.6 0.9 maximum_maximum_fusion.1
  147.6 8.6 %collective-permute-done.11 = bf16[2,18,28,128]{3,2,1,0:T(8,128)(2,1)S(1)} collective-permute-done((bf16[2,18,28,128]{3,2,1,0:T(8,128)(2,1)S(1)}, bf16[2,18,28,128]{3,2,1,0:T(8,128)(2,1)S(1)}, u32[]{:S(2)}, u32[]{:S(2)}) %collective-permute-start.11) | collective-permute-done | bytes 258080 | tf_op jit(solution)/shard_map/ppermute | solution.py:480
  156.3 0.1 maximum_maximum_fusion
  156.4 1.5 copy.48
  (55 shorter events, 0.4 us)
Async XLA Ops:
  0.6 14.9 %copy-start.4 = (bf16[4,28,28,128]{3,0,2,1:T(4,128)(2,1)S(1)}, bf16[4,28,28,128]{3,0,2,1:T(4,128)(2,1)}, u32[]{:S(2)}) copy-start(bf16[4,28,28,128]{3,0,2,1:T(4,128)(2,1)} %param.16) | copy-start | bytes 2408452
  1.5 26.5 %collective-permute-start.6 = (s32[4,14,28]{2,0,1:T(4,128)S(1)}, s32[4,14,28]{2,0,1:T(4,128)S(1)}, u32[]{:S(2)}, u32[]{:S(2)}) collective-permute-start(s32[4,14,28]{2,0,1:T(4,128)S(1)} %slice.91), channel_id=1, source_target_pairs={{0,240},{2,242},{4,244},{6,246},{8,248},{10,250},{12,252},{14,254}... | collective-permute-start | bytes 18824 | tf_op jit(solution)/shard_map/ppermute | solution.py:480
  9.9 5.9 %copy-start.5 = (bf16[4,7,7,512]{3,2,1,0:T(8,128)(2,1)}, bf16[4,7,7,512]{3,2,1,0:T(8,128)(2,1)S(1)}, u32[]{:S(2)}) copy-start(bf16[4,7,7,512]{3,2,1,0:T(8,128)(2,1)S(1)} %copy.45.cot) | copy-start | bytes 602116
  9.9 22.0 %collective-permute-start.3 = (bf16[2,4,7,512]{3,2,1,0:T(8,128)(2,1)S(1)}, bf16[2,4,7,512]{3,2,1,0:T(8,128)(2,1)S(1)}, u32[]{:S(2)}, u32[]{:S(2)}) collective-permute-start(bf16[2,4,7,512]{3,2,1,0:T(8,128)(2,1)S(1)} %slice.114), channel_id=1, source_target_pairs={{0,14},{2,0},{4,2},{6,4},{8,6},{10,8},{12,10},{14,12},{16,30},{18,... | collective-permute-start | bytes 172040 | tf_op jit(solution)/shard_map/ppermute | solution.py:480
  14.8 14.5 %collective-permute-start.5 = (bf16[2,3,7,512]{3,2,1,0:T(8,128)(2,1)S(1)}, bf16[2,3,7,512]{3,2,1,0:T(8,128)(2,1)S(1)}, u32[]{:S(2)}, u32[]{:S(2)}) collective-permute-start(bf16[2,3,7,512]{3,2,1,0:T(8,128)(2,1)S(1)} %get-tuple-element.18), channel_id=1, source_target_pairs={{0,254},{2,240},{4,242},{6,244},{8,246},{10,248},{12,250},{14,252}... | collective-permute-start | bytes 129032 | tf_op jit(solution)/shard_map/ppermute | solution.py:480
  14.9 17.0 %collective-permute-start.4 = (bf16[2,3,7,512]{3,2,1,0:T(8,128)(2,1)S(1)}, bf16[2,3,7,512]{3,2,1,0:T(8,128)(2,1)S(1)}, u32[]{:S(2)}, u32[]{:S(2)}) collective-permute-start(bf16[2,3,7,512]{3,2,1,0:T(8,128)(2,1)S(1)} %get-tuple-element.19), channel_id=1, source_target_pairs={{0,240},{2,242},{4,244},{6,246},{8,248},{10,250},{12,252},{14,254}... | collective-permute-start | bytes 129032 | tf_op jit(solution)/shard_map/ppermute | solution.py:480
  15.7 2.2 %copy-start.2 = (bf16[4,28,28,128]{3,2,1,0:T(8,128)(2,1)}, bf16[4,28,28,128]{3,2,1,0:T(8,128)(2,1)S(1)}, u32[]{:S(2)}) copy-start(bf16[4,28,28,128]{3,2,1,0:T(8,128)(2,1)S(1)} %copy.44.tokens) | copy-start | bytes 2408452
  15.7 2.0 %copy-start.8 = (s32[4,7,7]{2,0,1:T(4,128)S(1)}, s32[4,7,7]{2,0,1:T(4,128)}, u32[]{:S(2)}) copy-start(s32[4,7,7]{2,0,1:T(4,128)} %param.18) | copy-start | bytes 2356
  15.7 2.1 %copy-start.6 = (f32[1183,16]{0,1:T(8,128)S(1)}, f32[1183,16]{0,1:T(8,128)}, u32[]{:S(2)}) copy-start(f32[1183,16]{0,1:T(8,128)} %param.30) | copy-start | bytes 227140
  15.7 2.1 %copy-start.7 = (f32[1183,4]{0,1:T(4,128)S(1)}, f32[1183,4]{0,1:T(4,128)}, u32[]{:S(2)}) copy-start(f32[1183,4]{0,1:T(4,128)} %param.22) | copy-start | bytes 56788
  15.8 27.6 %collective-permute-start = (bf16[2,18,28,128]{3,2,1,0:T(8,128)(2,1)S(1)}, bf16[2,18,28,128]{3,2,1,0:T(8,128)(2,1)}, u32[]{:S(2)}, u32[]{:S(2)}) collective-permute-start(bf16[2,18,28,128]{3,2,1,0:T(8,128)(2,1)S(1)} %slice.111), channel_id=1, source_target_pairs={{0,14},{2,0},{4,2},{6,4},{8,6},{10,8},{12,10},{14,12},{16,30},{18,... | collective-permute-start | bytes 774152 | tf_op jit(solution)/shard_map/ppermute | solution.py:480
  17.9 7.5 %slice-start.1 = ((bf16[128,384]{1,0:T(8,128)(2,1)}), bf16[128,256]{1,0:T(8,128)(2,1)S(1)}, s32[]{:S(2)}) async-start(bf16[128,384]{1,0:T(8,128)(2,1)} %projection_one.1), calls=%async_computation.1 | async-start | bytes 131072 | tf_op jit(solution)/shard_map/slice | solution.py:539
  21.9 1.8 %copy-start = (f32[4,224,1024]{2,1,0:T(8,128)}, f32[4,224,1024]{2,1,0:T(8,128)S(1)}, u32[]{:S(2)}) copy-start(f32[4,224,1024]{2,1,0:T(8,128)S(1)} %get-tuple-element.7.bias_three) | copy-start | bytes 11010052
  23.7 1.0 copy-start.1
  25.4 1.2 slice-start
  26.6 1.3 slice-start.2
  27.9 7.1 %collective-permute-start.2 = (bf16[2,17,28,128]{3,2,1,0:T(8,128)(2,1)S(1)}, bf16[2,17,28,128]{3,2,1,0:T(8,128)(2,1)S(1)}, u32[]{:S(2)}, u32[]{:S(2)}) collective-permute-start(bf16[2,17,28,128]{3,2,1,0:T(8,128)(2,1)S(1)} %get-tuple-element.16), channel_id=1, source_target_pairs={{0,254},{2,240},{4,242},{6,244},{8,246},{10,248},{12,250},{14,252}... | collective-permute-start | bytes 731144 | tf_op jit(solution)/shard_map/ppermute | solution.py:480
  29.2 14.2 %copy-start.12 = (bf16[2,3,7,512]{3,2,1,0:T(8,128)(2,1)}, bf16[2,3,7,512]{3,2,1,0:T(8,128)(2,1)S(1)}, u32[]{:S(2)}) copy-start(bf16[2,3,7,512]{3,2,1,0:T(8,128)(2,1)S(1)} %collective-permute-done.5.cot_both) | copy-start | bytes 129028
  29.3 14.1 %collective-permute-start.1 = (bf16[2,17,28,128]{3,2,1,0:T(8,128)(2,1)S(1)}, bf16[2,17,28,128]{3,2,1,0:T(8,128)(2,1)S(1)}, u32[]{:S(2)}, u32[]{:S(2)}) collective-permute-start(bf16[2,17,28,128]{3,2,1,0:T(8,128)(2,1)S(1)} %get-tuple-element.17), channel_id=1, source_target_pairs={{0,240},{2,242},{4,244},{6,246},{8,248},{10,250},{12,252},{14,254}... | collective-permute-start | bytes 731144 | tf_op jit(solution)/shard_map/ppermute | solution.py:480
  31.9 11.5 %copy-start.13 = (bf16[2,3,7,512]{3,2,1,0:T(8,128)(2,1)}, bf16[2,3,7,512]{3,2,1,0:T(8,128)(2,1)S(1)}, u32[]{:S(2)}) copy-start(bf16[2,3,7,512]{3,2,1,0:T(8,128)(2,1)S(1)} %collective-permute-done.4.cot_ha) | copy-start | bytes 129028
  31.9 11.5 %copy-start.11 = (bf16[2,4,7,512]{3,2,1,0:T(8,128)(2,1)}, bf16[2,4,7,512]{3,2,1,0:T(8,128)(2,1)S(1)}, u32[]{:S(2)}) copy-start(bf16[2,4,7,512]{3,2,1,0:T(8,128)(2,1)S(1)} %collective-permute-done.3.cot_ta) | copy-start | bytes 172036
  35.0 8.4 %copy-start.9 = (bf16[2,17,28,128]{3,2,1,0:T(8,128)(2,1)}, bf16[2,17,28,128]{3,2,1,0:T(8,128)(2,1)S(1)}, u32[]{:S(2)}) copy-start(bf16[2,17,28,128]{3,2,1,0:T(8,128)(2,1)S(1)} %collective-permute-done.2.tokens_both) | copy-start | bytes 731140
  43.4 0.7 copy-start.10
  123.2 6.5 %copy-start.3 = (bf16[4,35,28,128]{3,2,1,0:T(8,128)(2,1)S(1)}, bf16[4,35,28,128]{3,2,1,0:T(8,128)(2,1)}, u32[]{:S(2)}) copy-start(bf16[4,35,28,128]{3,2,1,0:T(8,128)(2,1)} %get-tuple-element.9) | copy-start | bytes 3010564
  124.5 22.1 %collective-permute-start.8 = (bf16[2,4,7,512]{3,0,2,1:T(2,128)(2,1)S(1)}, bf16[2,4,7,512]{3,0,2,1:T(2,128)(2,1)S(1)}, u32[]{:S(2)}, u32[]{:S(2)}) collective-permute-start(bf16[2,4,7,512]{3,0,2,1:T(2,128)(2,1)S(1)} %get-tuple-element.22), channel_id=1, source_target_pairs={{0,2},{2,4},{4,6},{6,8},{8,10},{10,12},{12,14},{14,0},{16,18},{18,... | collective-permute-start | bytes 172040 | tf_op jit(solution)/shard_map/ppermute | solution.py:480
  127.0 20.5 %collective-permute-start.10 = (bf16[2,17,28,128]{3,2,1,0:T(8,128)(2,1)S(1)}, bf16[2,17,28,128]{3,2,1,0:T(8,128)(2,1)S(1)}, u32[]{:S(2)}, u32[]{:S(2)}) collective-permute-start(bf16[2,17,28,128]{3,2,1,0:T(8,128)(2,1)S(1)} %get-tuple-element.14), channel_id=1, source_target_pairs={{0,18},{2,20},{4,22},{6,24},{8,26},{10,28},{12,30},{14,16},{16,34}... | collective-permute-start | bytes 731144 | tf_op jit(solution)/shard_map/ppermute | solution.py:480
  127.1 20.4 %collective-permute-start.12 = (bf16[2,17,28,128]{3,2,1,0:T(8,128)(2,1)S(1)}, bf16[2,17,28,128]{3,2,1,0:T(8,128)(2,1)S(1)}, u32[]{:S(2)}, u32[]{:S(2)}) collective-permute-start(bf16[2,17,28,128]{3,2,1,0:T(8,128)(2,1)S(1)} %get-tuple-element.15), channel_id=1, source_target_pairs={{0,16},{2,18},{4,20},{6,22},{8,24},{10,26},{12,28},{14,30},{16,32}... | collective-permute-start | bytes 731144 | tf_op jit(solution)/shard_map/ppermute | solution.py:480
  129.6 17.0 %collective-permute-start.7 = (bf16[2,3,7,512]{3,0,2,1:T(2,128)(2,1)S(1)}, bf16[2,3,7,512]{3,0,2,1:T(2,128)(2,1)S(1)}, u32[]{:S(2)}, u32[]{:S(2)}) collective-permute-start(bf16[2,3,7,512]{3,0,2,1:T(2,128)(2,1)S(1)} %get-tuple-element.20), channel_id=1, source_target_pairs={{0,18},{2,20},{4,22},{6,24},{8,26},{10,28},{12,30},{14,16},{16,34}... | collective-permute-start | bytes 129032 | tf_op jit(solution)/shard_map/ppermute | solution.py:480
  129.8 16.8 %collective-permute-start.9 = (bf16[2,3,7,512]{3,0,2,1:T(2,128)(2,1)S(1)}, bf16[2,3,7,512]{3,0,2,1:T(2,128)(2,1)S(1)}, u32[]{:S(2)}, u32[]{:S(2)}) collective-permute-start(bf16[2,3,7,512]{3,0,2,1:T(2,128)(2,1)S(1)} %get-tuple-element.21), channel_id=1, source_target_pairs={{0,16},{2,18},{4,20},{6,22},{8,24},{10,26},{12,28},{14,30},{16,32}... | collective-permute-start | bytes 129032 | tf_op jit(solution)/shard_map/ppermute | solution.py:480
  146.6 9.6 %collective-permute-start.11 = (bf16[2,18,28,128]{3,2,1,0:T(8,128)(2,1)S(1)}, bf16[2,18,28,128]{3,2,1,0:T(8,128)(2,1)S(1)}, u32[]{:S(2)}, u32[]{:S(2)}) collective-permute-start(bf16[2,18,28,128]{3,2,1,0:T(8,128)(2,1)S(1)} %slice.103), channel_id=1, source_target_pairs={{0,2},{2,4},{4,6},{6,8},{8,10},{10,12},{12,14},{14,0},{16,18},{18,... | collective-permute-start | bytes 774152 | tf_op jit(solution)/shard_map/ppermute | solution.py:480
where the time goes:
time: 158 us
  Pallas kernels  82.1 us (52%)
  waiting for transfers between devices  36.9 us (23%)
  starting transfers between devices  20 us (13%)
  local copies, waits for them, and re-layouts  14.5 us (9%)
  other arithmetic  3.44 us (2%)
    pallas_call x1, Pallas kernels, main_call(): pl.pallas_call(main_kernel, out_shape=(jax.ShapeDtypeStruct((ROWS, C3), B...  78.1 us
    ppermute x13, waiting for transfers between devices, send(): return lax.ppermute(values, ('ha', 'ta'), pairs)  36.9 us
    ppermute x13, starting transfers between devices, send(): return lax.ppermute(values, ('ha', 'ta'), pairs)  20 us
    unnamed x37, local copies, waits for them, and re-layouts  8.36 us
    pallas_call x1, Pallas kernels, expand_tables(): pl.pallas_call(bias_kernel, out_shape=(jax.ShapeDtypeStruct((1, ROWS, 4 *...  3.92 us
  transfers between devices with their start and end apart: 13, of which 4 were waited for; matrix products, arithmetic and copies ran while one was open for 6% of the time, Pallas kernels for 2%

commit v1 on v0

--- a/solution.py
+++ b/solution.py
@@ -21,10 +21,10 @@
 GROUPS = 28
 ROWS = 224
 LANES = 256
-WINDOWS = 20
+WINDOWS = 16
 FIRST = 10
 OWN = 28 - FIRST
-NEXT = 35 - OWN
+CELLS = 48
 
 LOG2E = math.log2(math.e)
 LN2 = math.log(2.0)
@@ -70,9 +70,11 @@
     return jnp.concatenate([x, jnp.zeros((LANES - ROWS, x.shape[1]), x.dtype)], 0)
 
 
-def attend(q, k, values_t, hot, bias_ref, bias_at, probs_ref, at):
+def attend(q, k, values_t, hot, hot_at, bias_ref, bias_at, probs_ref, at):
     k_wide = jnp.concatenate([k, hot], 1)
-    apart = padded((hot - 1.0) * jnp.array(LEFT_OUT, BF16))
+    lane = lax.broadcasted_iota(jnp.int32, (1, 128), 1)
+    chosen = jnp.where((lane >= hot_at) & (lane < hot_at + 4), LEFT_OUT, 0.0).astype(BF16)
+    apart = padded((hot - 1.0) * chosen)
     q = padded(q)
     out = []
     for head in range(4):
@@ -111,7 +113,7 @@
     return jnp.concatenate([d_q.astype(BF16), (d_keys * LN2).astype(BF16), d_values.astype(BF16)], 1)
 
 
-def bias_kernel(table_ref, one_ref, three_ref, wide_ref):
+def expand_tables(table_ref, one_ref, three_ref, wide_ref):
     for head in range(ALL_HEADS):
         row = jnp.broadcast_to(table_ref[head : head + 1, :] * LOG2E, (8, TABLE_LANES))
         for frame in range(4):
@@ -146,49 +148,42 @@
                     three_ref[group_at, to, place * LANES : (place + 1) * LANES] = block
 
 
-def expand_tables(tables):
-    return pl.pallas_call(
-        bias_kernel,
-        out_shape=(
-            jax.ShapeDtypeStruct((1, ROWS, 4 * LANES), F32),
-            jax.ShapeDtypeStruct((4, ROWS, 4 * LANES), F32),
-        ),
-        in_specs=[pl.BlockSpec(memory_space=pltpu.VMEM)],
-        out_specs=(pl.BlockSpec(memory_space=pltpu.VMEM), pl.BlockSpec(memory_space=pltpu.VMEM)),
-        scratch_shapes=[pltpu.VMEM((4 * ALL_HEADS * 8, DEPTH), F32)],
-        compiler_params=pltpu.CompilerParams(vmem_limit_bytes=48 * 2**20),
-        cost_estimate=pl.CostEstimate(flops=4 * 10**9, bytes_accessed=6 * 10**6, transcendentals=0),
-        name="expand_tables",
-    )(tables)
-
-
 def main_kernel(
+    ha_count,
+    ta_count,
     tokens,
-    tokens_ta,
-    tokens_ha,
-    tokens_both,
-    cot,
-    cot_ta,
-    cot_ha,
-    cot_both,
-    hot_one,
-    hot_three,
+    cotangent,
+    hot_own,
+    tables,
+    gain_one,
+    projection_one,
+    outward_one,
+    merge_gain_one,
+    merge_weight_one_hbm,
+    merge_gain_two,
+    merge_weight_two_hbm,
+    gain_three,
+    projection_three_hbm,
+    outward_three_hbm,
+    section_out,
+    grad_out,
+    held,
+    cot_held,
+    hot,
+    seam_out,
+    seam_in,
+    back_out,
+    back_in,
+    section_stage,
+    grad_stage,
+    merge_weight_one,
+    merge_weight_two,
+    projection_three,
+    outward_three,
+    kv_one_t,
+    kv_three_t,
     bias_one,
     bias_three,
-    gain_one,
-    projection_one,
-    kv_one_t,
-    outward_one,
-    merge_gain_one,
-    merge_weight_one,
-    merge_gain_two,
-    merge_weight_two,
-    gain_three,
-    projection_three,
-    kv_three_t,
-    outward_three,
-    section_out,
-    grad_out,
     grid,
     folded,
     windows,
@@ -213,38 +208,100 @@
     d_out_t_three,
     d_packed_three,
     cot_wide,
+    wide,
+    send_sems,
+    receive_sems,
+    own_sems,
 ):
-    def place_row(frame, row, values):
-        values = values.astype(F32)
-        grid[frame, row, 0:28, :] = values
-        grid[frame, row, 28:36, :] = values[0:8]
-
-    def own_rows(row, _):
-        for frame in range(2):
-            place_row(frame, row, tokens[2 + frame, FIRST + row])
-            place_row(2 + frame, row, tokens_ta[frame, row])
-        return 0
-
-    def next_rows(row, _):
-        for frame in range(2):
-            place_row(frame, OWN + row, tokens_ha[frame, row])
-            place_row(2 + frame, OWN + row, tokens_both[frame, row])
-        return 0
-
-    lax.fori_loop(0, OWN, own_rows, 0)
-    lax.fori_loop(0, NEXT, next_rows, 0)
-
-    def cut(k, _):
-        for m in range(4):
-            for frame in range(4):
-                for row in range(7):
-                    group = (frame * 7 + row) * 8
-                    windows[4 * k + m, group : group + 8, :] = grid[frame, 7 * k + row, 3 + 7 * m : 11 + 7 * m, :]
-        return 0
-
-    lax.fori_loop(0, 5, cut, 0)
-
-    def forward_one(at, _):
+    ha, ta = lax.axis_index("ha"), lax.axis_index("ta")
+    ha_next, ha_last = lax.rem(ha + 1, ha_count), lax.rem(ha + ha_count - 1, ha_count)
+    ta_next, ta_last = lax.rem(ta + 1, ta_count), lax.rem(ta + ta_count - 1, ta_count)
+
+    barrier = pltpu.get_barrier_semaphore()
+    ahead = ({"ta": ta_next}, {"ha": ha_next}, {"ha": ha_next, "ta": ta_next})
+    behind = ({"ta": ta_last}, {"ha": ha_last}, {"ha": ha_last, "ta": ta_last})
+
+    sent = []
+
+    def remote(source, target, device):
+        at = len(sent)
+        sent.append(
+            pltpu.make_async_remote_copy(
+                src_ref=source,
+                dst_ref=target,
+                send_sem=send_sems.at[at],
+                recv_sem=receive_sems.at[at],
+                device_id=device,
+                device_id_type=pl.DeviceIdType.MESH,
+            )
+        )
+        return sent[-1]
+
+    moved = []
+
+    def local(source, target):
+        moved.append(pltpu.make_async_copy(source, target, own_sems.at[len(moved)]))
+        return moved[-1]
+
+    tokens_own = local(tokens.at[2:4, FIRST:28], held.at[0:2, 0:OWN])
+    cot_own = local(cotangent.at[2:4, 3:7], cot_held.at[0:2, 0:4])
+    hot_copy = local(hot_own, hot.at[0])
+    weights = [
+        local(projection_three_hbm, projection_three),
+        local(merge_weight_one_hbm, merge_weight_one),
+        local(merge_weight_two_hbm, merge_weight_two),
+        local(outward_three_hbm, outward_three),
+    ]
+    tokens_ta = remote(tokens.at[0:2, FIRST : FIRST + 7], held.at[2:4, 0:7], behind[0])
+    tokens_ta_rest = remote(tokens.at[0:2, FIRST + 7 : 28], held.at[2:4, 7:OWN], behind[0])
+    tokens_ha = remote(tokens.at[2:4, 0:FIRST], held.at[0:2, OWN:28], behind[1])
+    tokens_both = remote(tokens.at[0:2, 0:FIRST], held.at[2:4, OWN:28], behind[2])
+    hot_ha = remote(hot_own, hot.at[1], behind[1])
+    cot_ta = remote(cotangent.at[0:2, 3:7], cot_held.at[2:4, 0:4], behind[0])
+    cot_ha = remote(cotangent.at[2:4, 0:3], cot_held.at[0:2, 4:7], behind[1])
+    cot_both = remote(cotangent.at[0:2, 0:3], cot_held.at[2:4, 4:7], behind[2])
+    seam = remote(seam_out, seam_in, behind[1])
+    back = remote(back_out, back_in, ahead[1])
+    section_copies = [
+        remote(section_stage.at[2:4, 0:4], section_out.at[0:2, 3:7], ahead[0]),
+        remote(section_stage.at[0:2, 4:7], section_out.at[2:4, 0:3], ahead[1]),
+        remote(section_stage.at[2:4, 4:7], section_out.at[0:2, 0:3], ahead[2]),
+        local(section_stage.at[0:2, 0:4], section_out.at[2:4, 3:7]),
+    ]
+    grad_copies = {3: [], 2: [], 1: [], 0: []}
+    for k, low, high in ((3, 21, 28), (2, 18, 21)):
+        to = slice(low - OWN, high - OWN)
+        grad_copies[k].append(remote(grad_stage.at[2:4, low:high], grad_out.at[0:2, to], ahead[2]))
+        grad_copies[k].append(remote(grad_stage.at[0:2, low:high], grad_out.at[2:4, to], ahead[1]))
+    for k, low, high in ((2, 14, 18), (1, 7, 14), (0, 0, 7)):
+        to = slice(low + FIRST, high + FIRST)
+        grad_copies[k].append(remote(grad_stage.at[2:4, low:high], grad_out.at[0:2, to], ahead[0]))
+        grad_copies[k].append(local(grad_stage.at[0:2, low:high], grad_out.at[2:4, to]))
+
+    tokens_own.start()
+    for device in ahead + behind:
+        pl.semaphore_signal(barrier, inc=1, device_id=device, device_id_type=pl.DeviceIdType.MESH)
+    pl.semaphore_wait(barrier, 6)
+    for copy in (tokens_ta, tokens_both, tokens_ha, tokens_ta_rest, hot_ha, cot_ta, cot_both, cot_ha):
+        copy.start()
+    hot_copy.start()
+    for copy in weights:
+        copy.start()
+    cot_own.start()
+
+    expand_tables(tables, bias_one, bias_three, wide)
+    for part in range(2):
+        weight = projection_one[:, C1 * (part + 1) : C1 * (part + 2)].astype(F32)
+        kv_one_t[C1 * part : C1 * part + C1, :] = jnp.transpose(weight).astype(BF16)
+    weights[0].wait()
+    for part in range(8):
+        weight = projection_three[:, C3 + C1 * part : C3 + C1 * part + C1].astype(F32)
+        kv_three_t[C1 * part : C1 * part + C1, :] = jnp.transpose(weight).astype(BF16)
+    tokens_own.wait()
+    hot_copy.wait()
+
+    def forward_one(k, m):
+        at = 4 * k + m
         x = windows[at]
         hat, _unused = normalised(x)
         normed = (hat * gain_one[...]).astype(BF16)
@@ -254,15 +311,55 @@
         v_one[at] = packed[:, 2 * C1 :].astype(BF16)
         q_one[at] = q
         kt_one[at] = packed_t[:C1]
-        out_t = attend(q, packed[:, C1 : 2 * C1].astype(BF16), packed_t[C1:], hot_one[at], bias_one, 0, probs_one, at)
+        hot_at = 4 * (4 * lax.rem(k + 1, 4) + m)
+        out_t = attend(
+            q,
+            packed[:, C1 : 2 * C1].astype(BF16),
+            packed_t[C1:],
+            hot[k // 3],
+            hot_at,
+            bias_one,
+            0,
+            probs_one,
+            at,
+        )
         out_t_one[at] = out_t.astype(BF16)
         out = jnp.transpose(out_t)[:ROWS].astype(BF16)
         mixed[at] = rounded(x + rounded(dot(out, outward_one[...])))
-        return 0
-
-    lax.fori_loop(0, WINDOWS, forward_one, 0)
-
-    def uncut(k, _):
+
+    def forward_row(k, _):
+        @pl.when(k == 0)
+        def _():
+            tokens_ta.wait_recv()
+
+        @pl.when(k == 1)
+        def _():
+            tokens_ta_rest.wait_recv()
+
+        @pl.when(k == 2)
+        def _():
+            tokens_both.wait_recv()
+            tokens_ha.wait_recv()
+
+        @pl.when(k == 3)
+        def _():
+            hot_ha.wait_recv()
+
+        for frame in range(4):
+            for row in range(7):
+                values = held[frame, 7 * k + row].astype(F32)
+                grid[frame, row, 0:28, :] = values
+                grid[frame, row, 28:36, :] = values[0:8]
+                group = (frame * 7 + row) * 8
+                for m in range(4):
+                    windows[4 * k + m, group : group + 8, :] = grid[frame, row, 3 + 7 * m : 11 + 7 * m, :]
+
+        def one(m, _):
+            forward_one(k, m)
+            return 0
+
+        lax.fori_loop(0, 4, one, 0)
+
         for frame in range(4):
             for row in range(7):
                 group = (frame * 7 + row) * 8
@@ -272,9 +369,23 @@
                 folded[frame, 7 * k + row, 35:42, :] = second
                 folded[frame, 7 * k + row, 14:21, :] = mixed[4 * k + 2, group : group + 7, :]
                 folded[frame, 7 * k + row, 21:28, :] = mixed[4 * k + 3, group : group + 7, :]
+
+        @pl.when(k == 0)
+        def _():
+            for frame in range(4):
+                for row in range(2):
+                    seam_out[frame, row] = folded[frame, row].astype(BF16)
+            seam.start()
+
         return 0
 
-    lax.fori_loop(0, 5, uncut, 0)
+    lax.fori_loop(0, 4, forward_row, 0)
+    seam.wait_recv()
+    for frame in range(4):
+        for row in range(2):
+            folded[frame, 28 + row] = seam_in[frame, row].astype(F32)
+    for copy in weights[1:]:
+        copy.wait()
 
     def gather_blocks(frame, _):
         for row in range(7):
@@ -314,23 +425,28 @@
         vt_three[g] = packed_t[C3 + C1 * g : C3 + C1 * g + C1]
 
     def forward_three(g, _):
-        out_t = attend(q_three[g], k_three[g], vt_three[g], hot_three[...], bias_three, g, probs_three, g)
+        out_t = attend(q_three[g], k_three[g], vt_three[g], hot[0], 64, bias_three, g, probs_three, g)
         out_t_three[g] = out_t.astype(BF16)
         out_three[g] = jnp.transpose(out_t)[:ROWS].astype(BF16)
         return 0
 
     lax.fori_loop(0, 4, forward_three, 0)
     out = jnp.concatenate([out_three[g] for g in range(4)], 1)
-    section = merged_two + rounded(dot(out, outward_three[...]))
-    section_out[...] = section.astype(BF16)
-
+    cot_wide[...] = merged_two + rounded(dot(out, outward_three[...]))
     for frame in range(4):
         for row in range(7):
-            if row < 4:
-                source = cot[2 + frame, 3 + row] if frame < 2 else cot_ta[frame - 2, row]
-            else:
-                source = cot_ha[frame, row - 4] if frame < 2 else cot_both[frame - 2, row - 4]
-            source = source.astype(F32)
+            group = (frame * 7 + row) * 8
+            values = jnp.concatenate([cot_wide[group + 4 : group + 7, :], cot_wide[group : group + 4, :]], 0)
+            section_stage[frame, row] = values.astype(BF16)
+    for copy in section_copies:
+        copy.start()
+
+    cot_own.wait()
+    for copy in (cot_ta, cot_both, cot_ha):
+        copy.wait_recv()
+    for frame in range(4):
+        for row in range(7):
+            source = cot_held[frame, row].astype(F32)
             group = (frame * 7 + row) * 8
             cot_wide[group : group + 4, :] = source[3:7]
             cot_wide[group + 4 : group + 7, :] = source[0:3]
@@ -368,10 +484,6 @@
         d_grouped = dot_t(d_merged_one[:, 256 * place : 256 * place + 256], merge_weight_one[...])
         grouped[place] = norm_pull(d_grouped, grouped[place], inverse_one[place][:, :1], merge_gain_one[...])
 
-    for frame in range(4):
-        for row in (0, 1, 30, 31, 32, 33, 34):
-            folded[frame, row] = jnp.zeros((48, C1), F32)
-
     def scatter_blocks(frame, _):
         for row in range(7):
             group = (frame * 7 + row) * 8
@@ -386,20 +498,12 @@
         return 0
 
     lax.fori_loop(0, 4, scatter_blocks, 0)
-
-    def cut_back(k, _):
-        for frame in range(4):
-            for row in range(7):
-                group = (frame * 7 + row) * 8
-                folded[frame, 7 * k + row, 7:9, :] = folded[frame, 7 * k + row, 35:37, :]
-                mixed[4 * k, group : group + 8, :] = folded[frame, 7 * k + row, 28:36, :]
-                for m in range(1, 4):
-                    mixed[4 * k + m, group : group + 8, :] = folded[frame, 7 * k + row, 7 * m : 7 * m + 8, :]
-        return 0
-
-    lax.fori_loop(0, 5, cut_back, 0)
-
-    def backward_one(at, _):
+    for frame in range(4):
+        for row in range(2):
+            back_out[frame, row] = folded[frame, 28 + row].astype(BF16)
+    back.start()
+
+    def backward_one(at):
         hat, inverse = normalised(windows[at])
         d_residual = rounded(mixed[at])
         d_mixed = padded(d_residual.astype(BF16))
@@ -410,37 +514,93 @@
         )
         d_normed = rounded(dot_t(d_packed, projection_one[...]))
         mixed[at] = d_residual + norm_pull(d_normed, hat, inverse, gain_one[...])
-        return 0
-
-    lax.fori_loop(0, WINDOWS, backward_one, 0)
-
-    def place_back(k, _):
+
+    def backward_row(step, _):
+        k = 3 - step
+
+        @pl.when(k == 0)
+        def _():
+            back.wait_recv()
+            for frame in range(4):
+                for row in range(2):
+                    folded[frame, row] = back_in[frame, row].astype(F32)
+
+        for frame in range(4):
+            for row in range(7):
+                group = (frame * 7 + row) * 8
+                folded[frame, 7 * k + row, 7:9, :] = folded[frame, 7 * k + row, 35:37, :]
+                mixed[4 * k, group : group + 8, :] = folded[frame, 7 * k + row, 28:36, :]
+                for m in range(1, 4):
+                    mixed[4 * k + m, group : group + 8, :] = folded[frame, 7 * k + row, 7 * m : 7 * m + 8, :]
+
+        def one(m, _):
+            backward_one(4 * k + m)
+            return 0
+
+        lax.fori_loop(0, 4, one, 0)
+
         for frame in range(4):
             for row in range(7):
                 group = (frame * 7 + row) * 8
                 for m in range(3):
-                    grid[frame, 7 * k + row, 3 + 7 * m : 10 + 7 * m, :] = mixed[4 * k + m, group : group + 7, :]
-                grid[frame, 7 * k + row, 24:28, :] = mixed[4 * k + 3, group : group + 4, :]
-                grid[frame, 7 * k + row, 0:3, :] = mixed[4 * k + 3, group + 4 : group + 7, :]
-                grad_out[frame, 7 * k + row] = grid[frame, 7 * k + row, 0:28, :].astype(BF16)
+                    grid[frame, row, 3 + 7 * m : 10 + 7 * m, :] = mixed[4 * k + m, group : group + 7, :]
+                grid[frame, row, 24:28, :] = mixed[4 * k + 3, group : group + 4, :]
+                grid[frame, row, 0:3, :] = mixed[4 * k + 3, group + 4 : group + 7, :]
+                grad_stage[frame, 7 * k + row] = grid[frame, row, 0:28, :].astype(BF16)
+
+        for at in range(4):
+
+            @pl.when(k == at)
+            def _():
+                for copy in grad_copies[at]:
+                    copy.start()
+
         return 0
 
-    lax.fori_loop(0, 5, place_back, 0)
-
-
-def main_call(*operands):
+    lax.fori_loop(0, 4, backward_row, 0)
+
+    early = (tokens_ta, tokens_ta_rest, tokens_ha, tokens_both, hot_ha, cot_ta, cot_ha, cot_both, seam, back)
+    for copy in early:
+        copy.wait_send()
+    for copy in section_copies:
+        copy.wait()
+    for k in (3, 2, 1, 0):
+        for copy in grad_copies[k]:
+            copy.wait()
+
+
+def main_call(mesh_shape, *operands):
     vmem = pl.BlockSpec(memory_space=pltpu.VMEM)
+    hbm = pl.BlockSpec(memory_space=pl.ANY)
+    in_specs = [hbm, hbm, hbm, vmem, vmem, vmem, vmem, vmem, hbm, vmem, hbm, vmem, hbm, hbm]
     return pl.pallas_call(
-        main_kernel,
+        functools.partial(main_kernel, *mesh_shape),
         out_shape=(
-            jax.ShapeDtypeStruct((ROWS, C3), BF16),
-            jax.ShapeDtypeStruct((4, 35, 28, C1), BF16),
+            jax.ShapeDtypeStruct((4, 7, 7, C3), BF16),
+            jax.ShapeDtypeStruct((4, 28, 28, C1), BF16),
         ),
-        in_specs=[vmem] * len(operands),
-        out_specs=(vmem, vmem),
+        in_specs=in_specs,
+        out_specs=(hbm, hbm),
         scratch_shapes=[
-            pltpu.VMEM((4, 35, 40, C1), F32),
-            pltpu.VMEM((4, 35, 48, C1), F32),
+            pltpu.VMEM((4, 28, 28, C1), BF16),
+            pltpu.VMEM((4, 7, 7, C3), BF16),
+            pltpu.VMEM((2, ROWS, 128), BF16),
+            pltpu.VMEM((4, 2, CELLS, C1), BF16),
+            pltpu.VMEM((4, 2, CELLS, C1), BF16),
+            pltpu.VMEM((4, 2, CELLS, C1), BF16),
+            pltpu.VMEM((4, 2, CELLS, C1), BF16),
+            pltpu.VMEM((4, 7, 7, C3), BF16),
+            pltpu.VMEM((4, 28, 28, C1), BF16),
+            pltpu.VMEM((4 * C1, 2 * C1), BF16),
+            pltpu.VMEM((8 * C1, C3), BF16),
+            pltpu.VMEM((C3, 3 * C3), BF16),
+            pltpu.VMEM((C3, C3), BF16),
+            pltpu.VMEM((2 * C1, C1), BF16),
+            pltpu.VMEM((2 * C3, C3), BF16),
+            pltpu.VMEM((1, ROWS, 4 * LANES), F32),
+            pltpu.VMEM((4, ROWS, 4 * LANES), F32),
+            pltpu.VMEM((4, 7, 40, C1), F32),
+            pltpu.VMEM((4, 30, CELLS, C1), F32),
             pltpu.VMEM((WINDOWS, ROWS, C1), F32),
             pltpu.VMEM((WINDOWS, ROWS, C1), F32),
             pltpu.VMEM((WINDOWS, ROWS, 4 * LANES), BF16),
@@ -463,27 +623,24 @@
             pltpu.VMEM((4, C1, LANES), F32),
             pltpu.VMEM((4, ROWS, 3 * C1), BF16),
             pltpu.VMEM((ROWS, C3), F32),
+            pltpu.VMEM((4 * ALL_HEADS * 8, DEPTH), F32),
+            pltpu.SemaphoreType.DMA((20,)),
+            pltpu.SemaphoreType.DMA((20,)),
+            pltpu.SemaphoreType.DMA((12,)),
         ],
-        compiler_params=pltpu.CompilerParams(vmem_limit_bytes=60 * 2**20),
+        compiler_params=pltpu.CompilerParams(
+            vmem_limit_bytes=62 * 2**20, collective_id=0, has_side_effects=True
+        ),
         cost_estimate=pl.CostEstimate(flops=3 * 10**10, bytes_accessed=2 * 10**7, transcendentals=4 * 10**6),
         name="sections",
     )(*operands)
 
 
-def send(values, ha_by, ta_by):
-    ha_count, ta_count = lax.axis_size("ha"), lax.axis_size("ta")
-    pairs = []
-    for h in range(ha_count):
-        for t in range(ta_count):
-            to = ((h + ha_by) % ha_count) * ta_count + (t + ta_by) % ta_count
-            pairs.append((h * ta_count + t, to))
-    return lax.ppermute(values, ("ha", "ta"), pairs)
-
-
-def one_hot_regions(ids):
-    ids = jnp.pad(ids, ((0, 0), (0, 0), (0, 1)), constant_values=3)
-    ids = ids.reshape(-1, ROWS)
-    return (ids[:, :, None] == jnp.arange(128, dtype=jnp.int32)).astype(BF16)
+def region_classes(regions_one, regions_three):
+    ids = regions_one.reshape(4, 4, 7, 4, 7).transpose(0, 2, 4, 1, 3).reshape(4, 7, 7, WINDOWS)
+    ids = jnp.concatenate([ids, regions_three[:, :, :, None]], 3)
+    ids = jnp.pad(ids, ((0, 0), (0, 0), (0, 1), (0, 32 - WINDOWS - 1)), constant_values=3).reshape(ROWS, 32)
+    return (jnp.repeat(ids, 4, 1) == jnp.arange(128, dtype=jnp.int32) % 4).astype(BF16)
 
 
 def per_device(
@@ -504,39 +661,16 @@
     table_three,
     cotangent,
 ):
-    tokens_ta = send(tokens[:2, FIRST:], 0, -1)
-    tokens_ha = send(tokens[2:, :NEXT], -1, 0)
-    tokens_both = send(tokens[:2, :NEXT], -1, -1)
-    cot_ta = send(cotangent[:2, 3:], 0, -1)
-    cot_ha = send(cotangent[2:, :3], -1, 0)
-    cot_both = send(cotangent[:2, :3], -1, -1)
-    regions_next = send(regions_one[:, :14], -1, 0)
-
     tables = jnp.concatenate([table_one, table_three], 1).T
     tables = jnp.pad(tables, ((0, 0), (8, TABLE_LANES - 8 - tables.shape[1])))
-    bias_one, bias_three = expand_tables(tables)
-
-    ids = jnp.concatenate([regions_one[:, 7:], regions_next], 1)
-    ids = ids.reshape(4, 5, 7, 4, 7).transpose(1, 3, 0, 2, 4).reshape(WINDOWS, GROUPS, 7)
-    hot_one = one_hot_regions(ids)
-    hot_three = one_hot_regions(regions_three.reshape(1, GROUPS, 7))[0]
-
-    section, grad = main_call(
+    return main_call(
+        (lax.axis_size("ha"), lax.axis_size("ta")),
         tokens,
-        tokens_ta,
-        tokens_ha,
-        tokens_both,
         cotangent,
-        cot_ta,
-        cot_ha,
-        cot_both,
-        hot_one,
-        hot_three,
-        bias_one,
-        bias_three,
+        region_classes(regions_one, regions_three),
+        tables,
         gain_one.reshape(1, -1),
         projection_one,
-        projection_one[:, C1:].T,
         outward_one,
         merge_gain_one.reshape(1, -1),
         merge_weight_one,
@@ -544,29 +678,8 @@
         merge_weight_two,
         gain_three.reshape(1, -1),
         projection_three,
-        projection_three[:, C3:].T,
         outward_three,
     )
-
-    section = section.reshape(4, 7, 8, C3)
-    section = jnp.concatenate([section[:, :, 4:7], section[:, :, :4]], 2)
-    from_ta = send(section[2:, :4], 0, 1)
-    from_ha = send(section[:2, 4:], 1, 0)
-    from_both = send(section[2:, 4:], 1, 1)
-    finished = jnp.concatenate(
-        [jnp.concatenate([from_both, from_ta], 1), jnp.concatenate([from_ha, section[:2, :4]], 1)], 0
-    )
-
-    grad_ta = send(grad[2:, :OWN], 0, 1)
-    grad_ha = send(grad[:2, OWN:], 1, 0)
-    grad_both = send(grad[2:, OWN:], 1, 1)
-
-    def joined(behind, own):
-        shared = behind[:, FIRST:].astype(F32) + own[:, : NEXT - FIRST].astype(F32)
-        return jnp.concatenate([behind[:, :FIRST], shared.astype(BF16), own[:, NEXT - FIRST :]], 1)
-
-    grad_total = jnp.concatenate([joined(grad_both, grad_ta), joined(grad_ha, grad[:2, :OWN])], 0)
-    return (finished, grad_total)
 
 
 def solution(mesh):

time: 158 us -> 98.6 us (0.62)
  waiting for transfers between devices: 36.9 us -> 0 us
  starting transfers between devices: 20 us -> 0 us
  local copies, waits for them, and re-layouts: 14.5 us -> 9.54 us
  Pallas kernels: 82.1 us -> 85.7 us
  other arithmetic: 3.44 us -> 1.72 us
    ppermute x13 -> x0, waiting for transfers between devices: 36.9 us -> none  [send(): return lax.ppermute(values, ('ha', 'ta'), pairs)]
    ppermute x13 -> x0, starting transfers between devices: 20 us -> none  [send(): return lax.ppermute(values, ('ha', 'ta'), pairs)]
    unnamed x37 -> x7, local copies, waits for them, and re-layouts: 8.36 us -> 1.81 us
    slice x21 -> x0, local copies, waits for them, and re-layouts: 4.78 us -> none  [the longest x2 2.06 us: per_device(): section = jnp.concatenate([section[:, :, 4:7], section[:, :, :4]], 2)]
    pallas_call x0 -> x2, local copies, waits for them, and re-layouts: none -> 4.41 us  [main_call(): pl.pallas_call(functools.partial(main_kernel, *mesh_shape), out_shape=(ja...]
    pallas_call x2 -> x1, Pallas kernels: 82.1 us -> 85.7 us  [main_call(): pl.pallas_call(functools.partial(main_kernel, *mesh_shape), out_shape=(ja...]
    convert_element_type x4 -> x1, other arithmetic: 2.36 us -> 0.65 us  [region_classes(): (jnp.repeat(ids, 4, 1) == jnp.arange(128, dtype=jnp.int32) % 4).astype(BF16)]
  transfers between devices with their start and end apart: 13 -> 0, of which waited for: 4 -> 0; matrix products, arithmetic and copies ran while one was open for 6% -> 0% of each run, Pallas kernels for 2% -> 0%
where the time goes in v1:
time: 98.6 us; the launch traced here: 97.7 us
  Pallas kernels  85.7 us (87%)
  local copies, waits for them, and re-layouts  9.54 us (10%)
  other arithmetic  1.72 us (2%)
    pallas_call x1, Pallas kernels, main_call(): pl.pallas_call(functools.partial(main_kernel, *mesh_shape), out_shape=(ja...  85.7 us
    pallas_call x2, local copies, waits for them, and re-layouts, main_call(): pl.pallas_call(functools.partial(main_kernel, *mesh_shape), out_shape=(ja...  4.41 us

profile of v1, /device:TPU:1, one launch (start us, length us, event | category | flops | bytes accessed | tf_op | source)
XLA Modules:
  0.0 97.7 jit_solution(364038225815597048)
XLA Ops:
  0.6 1.0 %copy.41 = s32[4,7,7,1]{3,0,2,1:T(4,128)S(1)} copy(s32[4,7,7,1]{2,0,1,3:T(4,128)} %bitcast.17) | data formatting | bytes 1568 | tf_op jit(solution)/shard_map/broadcast_in_dim | solution.py:641
  1.6 0.9 maximum_bitcast_fusion
  2.5 0.0 copy-start.1
  2.6 0.8 pad.9.tables
  3.3 0.0 copy-start
  3.3 1.1 %reshape.37 = s32[4,4,7,4,7]{4,3,0,2,1:T(4,128)S(1)} reshape(s32[4,28,28]{2,0,1:T(4,128)} %param.17) | data formatting | bytes 25088 | tf_op jit(solution)/shard_map/reshape | solution.py:640
  4.4 0.2 copy.40
  4.7 0.2 pad_add_fusion
  4.9 0.1 copy.43
  5.0 0.1 copy.44
  5.1 0.7 compare_convert_fusion.hot_own
  5.8 0.0 copy-done.1
  5.8 0.7 copy.46.cotangent
  6.5 0.0 copy-done
  6.5 1.1 %copy.45.tokens = bf16[4,28,28,128]{3,2,1,0:T(8,128)(2,1)} copy(bf16[4,28,28,128]{3,0,2,1:T(4,128)(2,1)S(1)} %copy-done) | data formatting | bytes 1605632 | tf_op args[0]
  7.6 85.7 %sections.1 = (bf16[4,7,7,512]{3,2,1,0:T(8,128)(2,1)}, bf16[4,28,28,128]{3,2,1,0:T(8,128)(2,1)}) custom-call(bf16[4,28,28,128]{3,2,1,0:T(8,128)(2,1)} %copy.45.tokens, bf16[4,7,7,512]{3,2,1,0:T(8,128)(2,1)} %copy.46.cotangent, bf16[224,128]{1,0:T(8,128)(2,1)} %compare_convert_fusion.hot_own, f32[20,1408]{1,0:T(8,128)} %pad.9.tables, f32[1,128]{1,0:T(1,128)} %bitcast.21, ...), custom_call_target="tpu_custom_call" | custom-call | flops 30000001024 | bytes 20000000 | tf_op jit(solution)/shard_map/sections/pallas_call | solution.py:576
  93.3 1.7 %copy.47 = bf16[4,7,7,512]{3,0,2,1:T(4,128)(2,1)} copy(bf16[4,7,7,512]{3,2,1,0:T(8,128)(2,1)} %get-tuple-element.8) | data formatting | bytes 401408 | tf_op jit(solution)/shard_map/sections/pallas_call | solution.py:576
  95.0 2.7 %copy.48 = bf16[4,28,28,128]{3,0,2,1:T(4,128)(2,1)} copy(bf16[4,28,28,128]{3,2,1,0:T(8,128)(2,1)} %get-tuple-element.9) | data formatting | bytes 1605632 | tf_op jit(solution)/shard_map/sections/pallas_call | solution.py:576
  (6 shorter events, 0.2 us)
Async XLA Ops:
  2.5 3.2 %copy-start.1 = (bf16[4,7,7,512]{3,0,2,1:T(4,128)(2,1)S(1)}, bf16[4,7,7,512]{3,0,2,1:T(4,128)(2,1)}, u32[]{:S(2)}) copy-start(bf16[4,7,7,512]{3,0,2,1:T(4,128)(2,1)} %param.31) | copy-start | bytes 602116
  3.3 3.2 %copy-start = (bf16[4,28,28,128]{3,0,2,1:T(4,128)(2,1)S(1)}, bf16[4,28,28,128]{3,0,2,1:T(4,128)(2,1)}, u32[]{:S(2)}) copy-start(bf16[4,28,28,128]{3,0,2,1:T(4,128)(2,1)} %param.16) | copy-start | bytes 2408452

commit v2 on v1

--- a/solution.py
+++ b/solution.py
@@ -32,6 +32,7 @@
 LEFT_OUT = 1e30
 
 TABLE_LANES = 1408
+OFFSETS = 1183
 DEPTH = 768
 ALL_HEADS = HEADS1 + HEADS3
 
@@ -71,51 +72,59 @@
 
 
 def attend(q, k, values_t, hot, hot_at, bias_ref, bias_at, probs_ref, at):
-    k_wide = jnp.concatenate([k, hot], 1)
     lane = lax.broadcasted_iota(jnp.int32, (1, 128), 1)
     chosen = jnp.where((lane >= hot_at) & (lane < hot_at + 4), LEFT_OUT, 0.0).astype(BF16)
-    apart = padded((hot - 1.0) * chosen)
-    q = padded(q)
+    q_wide = jnp.concatenate([padded(q), padded((hot - 1.0) * chosen)], 1)
+    k_wide = jnp.concatenate([jnp.concatenate([k * head_mask(head), hot], 1) for head in range(4)], 0)
+    scores = dot_t(k_wide, q_wide)
     out = []
     for head in range(4):
-        q_wide = jnp.concatenate([q * head_mask(head), apart], 1)
-        scores = dot_t(k_wide, q_wide)
+        rows = slice(ROWS * head, ROWS * head + ROWS)
         for half in range(2):
             lanes = slice(128 * half, 128 * half + 128)
-            place = slice(LANES * head + 128 * half, LANES * head + 128 * half + 128)
-            part = scores[:, lanes] + bias_ref[bias_at, :, place]
+            part = scores[rows, lanes] + bias_ref[bias_at, rows, lanes]
             raised = jnp.exp2(part - jnp.max(part, 0, keepdims=True))
             share = 1.0 / jnp.sum(raised, 0, keepdims=True)
-            probs_ref[at, :, place] = (raised * share).astype(BF16)
-        probs = probs_ref[at, :, LANES * head : LANES * head + LANES]
-        out.append(dot(values_t[HEAD * head : HEAD * head + HEAD], probs))
+            probs_ref[at, rows, lanes] = (raised * share).astype(BF16)
+        out.append(dot(values_t[HEAD * head : HEAD * head + HEAD], probs_ref[at, rows, :]))
     return jnp.concatenate(out, 0)
 
 
 def attend_pull(d_out, d_out_t, out_t, q, keys_t, values, probs_ref, at):
     product = d_out_t * out_t
-    q = padded(q)
-    d_values = jnp.zeros((ROWS, C1), F32)
-    d_keys = jnp.zeros((ROWS, C1), F32)
+    values = jnp.concatenate([values * head_mask(head) for head in range(4)], 0)
+    d_probs = dot_t(values, d_out)
     d_queries = []
+    d_scores = []
     for head in range(4):
-        rows = slice(HEAD * head, HEAD * head + HEAD)
-        mask = head_mask(head)
-        d_head = d_out * mask
-        probs = probs_ref[at, :, LANES * head : LANES * head + LANES]
-        d_probs = dot_t(values, d_head)
-        delta = jnp.sum(product[rows], 0, keepdims=True)
-        d_scores = (probs.astype(F32) * (d_probs - delta)).astype(BF16)
-        d_values += dot(probs, d_head)
-        d_keys += dot(d_scores, q * mask)
-        d_queries.append(dot(keys_t[rows], d_scores))
+        rows = slice(ROWS * head, ROWS * head + ROWS)
+        own = slice(HEAD * head, HEAD * head + HEAD)
+        delta = jnp.sum(product[own], 0, keepdims=True)
+        d_scores.append((probs_ref[at, rows, :].astype(F32) * (d_probs[rows] - delta)).astype(BF16))
+        d_queries.append(dot(keys_t[own], d_scores[head]))
+    all_values = dot(probs_ref[at], d_out)
+    all_keys = dot(jnp.concatenate(d_scores, 0), padded(q))
+    d_values = pick_heads(all_values)
+    d_keys = pick_heads(all_keys) * LN2
     d_q = jnp.transpose(jnp.concatenate(d_queries, 0) * SCALE)[:ROWS]
-    return jnp.concatenate([d_q.astype(BF16), (d_keys * LN2).astype(BF16), d_values.astype(BF16)], 1)
-
-
-def expand_tables(table_ref, one_ref, three_ref, wide_ref):
+    return jnp.concatenate([d_q.astype(BF16), d_keys.astype(BF16), d_values.astype(BF16)], 1)
+
+
+def pick_heads(stacked):
+    lane = lax.broadcasted_iota(jnp.int32, (1, C1), 1)
+    result = stacked[3 * ROWS :]
+    for head in (2, 1, 0):
+        result = jnp.where(lane < HEAD * (head + 1), stacked[ROWS * head : ROWS * head + ROWS], result)
+    return result
+
+
+def expand_tables(table_one, table_three, one_ref, three_ref, table_ref, wide_ref):
+    table_ref[...] = jnp.zeros((24, TABLE_LANES), F32)
+    table_ref[0:HEADS1, 8 : 8 + OFFSETS] = table_one[...]
+    table_ref[8:24, 8 : 8 + OFFSETS] = table_three[...]
     for head in range(ALL_HEADS):
-        row = jnp.broadcast_to(table_ref[head : head + 1, :] * LOG2E, (8, TABLE_LANES))
+        held_at = head if head < HEADS1 else head + 8 - HEADS1
+        row = jnp.broadcast_to(table_ref[held_at : held_at + 1, :] * LOG2E, (8, TABLE_LANES))
         for frame in range(4):
             start = 14 + 169 * (3 - frame)
             moved = pltpu.roll(row, TABLE_LANES - start, 1, stride=1, stride_axis=0)
@@ -137,15 +146,35 @@
         chosen = jnp.where(chosen, 1.0, 0.0).astype(BF16)
         picked = dot(high, chosen) + dot(low, chosen)
         for key_frame in range(4):
-            to = slice(key_frame * 56 + key_line * 8, key_frame * 56 + key_line * 8 + 8)
+            to = key_frame * 56 + key_line * 8
             for head in range(ALL_HEADS):
                 first = (key_frame * ALL_HEADS + head) * 8
                 block = picked[first : first + 8]
                 if head < HEADS1:
-                    one_ref[0, to, head * LANES : (head + 1) * LANES] = block
+                    one_ref[0, head * ROWS + to : head * ROWS + to + 8, :] = block
                 else:
                     group_at, place = divmod(head - HEADS1, 4)
-                    three_ref[group_at, to, place * LANES : (place + 1) * LANES] = block
+                    three_ref[group_at, place * ROWS + to : place * ROWS + to + 8, :] = block
+
+
+def region_classes(one_ref, three_ref, hot_ref):
+    def spread(ref, first, width, lane_of):
+        place = lax.broadcasted_iota(jnp.int32, (8, width), 0)
+        column = lax.broadcasted_iota(jnp.int32, (8, width), 1)
+        own = jnp.where(column - 7 * ((column * 37) >> 8) == place, 1.0, 0.0)
+        ids = [ref[first + row, frame : frame + 1, :].astype(F32) * own for frame in range(4) for row in range(7)]
+        column = lax.broadcasted_iota(jnp.int32, (width, 128), 0)
+        lane = lax.broadcasted_iota(jnp.int32, (width, 128), 1)
+        target = jnp.where((lane >> 2) == lane_of + ((column * 37) >> 8), 1.0, 0.0).astype(BF16)
+        return dot(jnp.concatenate(ids, 0).astype(BF16), target)
+
+    ids = spread(three_ref, 0, 7, WINDOWS)
+    for k in range(4):
+        ids += spread(one_ref, 7 * k, 28, 4 * k)
+    lane = lax.broadcasted_iota(jnp.int32, (ROWS, 128), 1) & 3
+    place = lax.broadcasted_iota(jnp.int32, (ROWS, 128), 0) & 7
+    ids = jnp.where(place == 7, 3.0, ids)
+    hot_ref[0] = jnp.where(ids == lane.astype(F32), 1.0, 0.0).astype(BF16)
 
 
 def main_kernel(
@@ -153,8 +182,10 @@
     ta_count,
     tokens,
     cotangent,
-    hot_own,
-    tables,
+    regions_one,
+    regions_three,
+    table_one,
+    table_three,
     gain_one,
     projection_one,
     outward_one,
@@ -208,6 +239,7 @@
     d_out_t_three,
     d_packed_three,
     cot_wide,
+    tables,
     wide,
     send_sems,
     receive_sems,
@@ -245,7 +277,6 @@
 
     tokens_own = local(tokens.at[2:4, FIRST:28], held.at[0:2, 0:OWN])
     cot_own = local(cotangent.at[2:4, 3:7], cot_held.at[0:2, 0:4])
-    hot_copy = local(hot_own, hot.at[0])
     weights = [
         local(projection_three_hbm, projection_three),
         local(merge_weight_one_hbm, merge_weight_one),
@@ -256,7 +287,7 @@
     tokens_ta_rest = remote(tokens.at[0:2, FIRST + 7 : 28], held.at[2:4, 7:OWN], behind[0])
     tokens_ha = remote(tokens.at[2:4, 0:FIRST], held.at[0:2, OWN:28], behind[1])
     tokens_both = remote(tokens.at[0:2, 0:FIRST], held.at[2:4, OWN:28], behind[2])
-    hot_ha = remote(hot_own, hot.at[1], behind[1])
+    hot_ha = remote(hot.at[0], hot.at[1], behind[1])
     cot_ta = remote(cotangent.at[0:2, 3:7], cot_held.at[2:4, 0:4], behind[0])
     cot_ha = remote(cotangent.at[2:4, 0:3], cot_held.at[0:2, 4:7], behind[1])
     cot_both = remote(cotangent.at[0:2, 0:3], cot_held.at[2:4, 4:7], behind[2])
@@ -282,14 +313,15 @@
     for device in ahead + behind:
         pl.semaphore_signal(barrier, inc=1, device_id=device, device_id_type=pl.DeviceIdType.MESH)
     pl.semaphore_wait(barrier, 6)
-    for copy in (tokens_ta, tokens_both, tokens_ha, tokens_ta_rest, hot_ha, cot_ta, cot_both, cot_ha):
+    for copy in (tokens_ta, tokens_both, tokens_ha, tokens_ta_rest, cot_ta, cot_both, cot_ha):
         copy.start()
-    hot_copy.start()
     for copy in weights:
         copy.start()
     cot_own.start()
 
-    expand_tables(tables, bias_one, bias_three, wide)
+    region_classes(regions_one, regions_three, hot)
+    hot_ha.start()
+    expand_tables(table_one, table_three, bias_one, bias_three, tables, wide)
     for part in range(2):
         weight = projection_one[:, C1 * (part + 1) : C1 * (part + 2)].astype(F32)
         kv_one_t[C1 * part : C1 * part + C1, :] = jnp.transpose(weight).astype(BF16)
@@ -298,7 +330,6 @@
         weight = projection_three[:, C3 + C1 * part : C3 + C1 * part + C1].astype(F32)
         kv_three_t[C1 * part : C1 * part + C1, :] = jnp.transpose(weight).astype(BF16)
     tokens_own.wait()
-    hot_copy.wait()
 
     def forward_one(k, m):
         at = 4 * k + m
@@ -358,7 +389,7 @@
             forward_one(k, m)
             return 0
 
-        lax.fori_loop(0, 4, one, 0)
+        lax.fori_loop(0, 4, one, 0, unroll=4)
 
         for frame in range(4):
             for row in range(7):
@@ -430,7 +461,7 @@
         out_three[g] = jnp.transpose(out_t)[:ROWS].astype(BF16)
         return 0
 
-    lax.fori_loop(0, 4, forward_three, 0)
+    lax.fori_loop(0, 4, forward_three, 0, unroll=4)
     out = jnp.concatenate([out_three[g] for g in range(4)], 1)
     cot_wide[...] = merged_two + rounded(dot(out, outward_three[...]))
     for frame in range(4):
@@ -472,7 +503,7 @@
         )
         return 0
 
-    lax.fori_loop(0, 4, backward_three, 0)
+    lax.fori_loop(0, 4, backward_three, 0, unroll=4)
     d_packed = jnp.concatenate(
         [d_packed_three[g, :, C1 * part : C1 * part + C1] for part in range(3) for g in range(4)], 1
     )
@@ -537,7 +568,7 @@
             backward_one(4 * k + m)
             return 0
 
-        lax.fori_loop(0, 4, one, 0)
+        lax.fori_loop(0, 4, one, 0, unroll=4)
 
         for frame in range(4):
             for row in range(7):
@@ -572,7 +603,7 @@
 def main_call(mesh_shape, *operands):
     vmem = pl.BlockSpec(memory_space=pltpu.VMEM)
     hbm = pl.BlockSpec(memory_space=pl.ANY)
-    in_specs = [hbm, hbm, hbm, vmem, vmem, vmem, vmem, vmem, hbm, vmem, hbm, vmem, hbm, hbm]
+    in_specs = [hbm, hbm, vmem, vmem, vmem, vmem, vmem, vmem, vmem, vmem, hbm, vmem, hbm, vmem, hbm, hbm]
     return pl.pallas_call(
         functools.partial(main_kernel, *mesh_shape),
         out_shape=(
@@ -597,13 +628,13 @@
             pltpu.VMEM((C3, C3), BF16),
             pltpu.VMEM((2 * C1, C1), BF16),
             pltpu.VMEM((2 * C3, C3), BF16),
-            pltpu.VMEM((1, ROWS, 4 * LANES), F32),
-            pltpu.VMEM((4, ROWS, 4 * LANES), F32),
+            pltpu.VMEM((1, 4 * ROWS, LANES), F32),
+            pltpu.VMEM((4, 4 * ROWS, LANES), F32),
             pltpu.VMEM((4, 7, 40, C1), F32),
             pltpu.VMEM((4, 30, CELLS, C1), F32),
             pltpu.VMEM((WINDOWS, ROWS, C1), F32),
             pltpu.VMEM((WINDOWS, ROWS, C1), F32),
-            pltpu.VMEM((WINDOWS, ROWS, 4 * LANES), BF16),
+            pltpu.VMEM((WINDOWS, 4 * ROWS, LANES), BF16),
             pltpu.VMEM((WINDOWS, ROWS, C1), BF16),
             pltpu.VMEM((WINDOWS, C1, ROWS), BF16),
             pltpu.VMEM((WINDOWS, ROWS, C1), BF16),
@@ -611,7 +642,7 @@
             pltpu.VMEM((4, ROWS, 512), F32),
             pltpu.VMEM((4, ROWS, 128), F32),
             pltpu.VMEM((ROWS, 1024), F32),
-            pltpu.VMEM((4, ROWS, 4 * LANES), BF16),
+            pltpu.VMEM((4, 4 * ROWS, LANES), BF16),
             pltpu.VMEM((4, ROWS, C1), BF16),
             pltpu.VMEM((4, ROWS, C1), BF16),
             pltpu.VMEM((4, ROWS, C1), BF16),
@@ -623,6 +654,7 @@
             pltpu.VMEM((4, C1, LANES), F32),
             pltpu.VMEM((4, ROWS, 3 * C1), BF16),
             pltpu.VMEM((ROWS, C3), F32),
+            pltpu.VMEM((24, TABLE_LANES), F32),
             pltpu.VMEM((4 * ALL_HEADS * 8, DEPTH), F32),
             pltpu.SemaphoreType.DMA((20,)),
             pltpu.SemaphoreType.DMA((20,)),
@@ -634,13 +666,6 @@
         cost_estimate=pl.CostEstimate(flops=3 * 10**10, bytes_accessed=2 * 10**7, transcendentals=4 * 10**6),
         name="sections",
     )(*operands)
-
-
-def region_classes(regions_one, regions_three):
-    ids = regions_one.reshape(4, 4, 7, 4, 7).transpose(0, 2, 4, 1, 3).reshape(4, 7, 7, WINDOWS)
-    ids = jnp.concatenate([ids, regions_three[:, :, :, None]], 3)
-    ids = jnp.pad(ids, ((0, 0), (0, 0), (0, 1), (0, 32 - WINDOWS - 1)), constant_values=3).reshape(ROWS, 32)
-    return (jnp.repeat(ids, 4, 1) == jnp.arange(128, dtype=jnp.int32) % 4).astype(BF16)
 
 
 def per_device(
@@ -661,14 +686,14 @@
     table_three,
     cotangent,
 ):
-    tables = jnp.concatenate([table_one, table_three], 1).T
-    tables = jnp.pad(tables, ((0, 0), (8, TABLE_LANES - 8 - tables.shape[1])))
     return main_call(
         (lax.axis_size("ha"), lax.axis_size("ta")),
         tokens,
         cotangent,
-        region_classes(regions_one, regions_three),
-        tables,
+        regions_one.transpose(1, 0, 2),
+        regions_three.transpose(1, 0, 2),
+        table_one.T,
+        table_three.T,
         gain_one.reshape(1, -1),
         projection_one,
         outward_one,

time: 98.6 us -> 75.6 us (0.77)
  Pallas kernels: 85.7 us -> 66.4 us
  other arithmetic: 1.72 us -> 0 us
  local copies, waits for them, and re-layouts: 9.54 us -> 8.28 us
    pallas_call x1, Pallas kernels: 85.7 us -> 66.4 us  [main_call(): pl.pallas_call(functools.partial(main_kernel, *mesh_shape), out_shape=(ja...]
    unnamed x7 -> x2, local copies, waits for them, and re-layouts: 1.81 us -> 3.87 us
    reshape x6 -> x0, local copies, waits for them, and re-layouts: 1.51 us -> none  [the longest x3 1.32 us: region_classes(): regions_one.reshape(4, 4, 7, 4, 7).transpose(0, 2, 4, 1, 3)]
    broadcast_in_dim x2 -> x0, local copies, waits for them, and re-layouts: 1.02 us -> none  [the longest x1 0.99 us: region_classes(): ids = jnp.concatenate([ids, regions_three[:, :, :, None]], 3)]
where the time goes in v2:
time: 75.6 us; the launch traced here: 75.3 us
  Pallas kernels  66.4 us (88%)
  local copies, waits for them, and re-layouts  8.28 us (11%)
    pallas_call x1, Pallas kernels, main_call(): pl.pallas_call(functools.partial(main_kernel, *mesh_shape), out_shape=(ja...  66.4 us
    pallas_call x2, local copies, waits for them, and re-layouts, main_call(): pl.pallas_call(functools.partial(main_kernel, *mesh_shape), out_shape=(ja...  4.41 us
    unnamed x2, local copies, waits for them, and re-layouts  3.87 us

profile of v2, /device:TPU:1, one launch (start us, length us, event | category | flops | bytes accessed | tf_op | source)
XLA Modules:
  0.0 75.3 jit_solution(3460357553237361614)
XLA Ops:
  0.6 1.7 %copy.19.cotangent = bf16[4,7,7,512]{3,2,1,0:T(8,128)(2,1)} copy(bf16[4,7,7,512]{3,0,2,1:T(4,128)(2,1)} %param.31) | data formatting | bytes 401408 | tf_op args[15]
  2.3 2.2 %copy.18.tokens = bf16[4,28,28,128]{3,2,1,0:T(8,128)(2,1)} copy(bf16[4,28,28,128]{3,0,2,1:T(4,128)(2,1)} %param.16) | data formatting | bytes 1605632 | tf_op args[0]
  4.5 66.4 %sections.1 = (bf16[4,7,7,512]{3,2,1,0:T(8,128)(2,1)}, bf16[4,28,28,128]{3,2,1,0:T(8,128)(2,1)}) custom-call(bf16[4,28,28,128]{3,2,1,0:T(8,128)(2,1)} %copy.18.tokens, bf16[4,7,7,512]{3,2,1,0:T(8,128)(2,1)} %copy.19.cotangent, s32[28,4,28]{2,1,0:T(4,128)} %bitcast.9, s32[7,4,7]{2,1,0:T(4,128)} %bitcast.11, f32[4,1183]{1,0:T(4,128)} %bitcast.10, ...), custom_call_target="tpu_custom_call" | custom-call | flops 30000001024 | bytes 20000000 | tf_op jit(solution)/shard_map/sections/pallas_call | solution.py:607
  70.9 1.7 %copy.20 = bf16[4,7,7,512]{3,0,2,1:T(4,128)(2,1)} copy(bf16[4,7,7,512]{3,2,1,0:T(8,128)(2,1)} %get-tuple-element.2) | data formatting | bytes 401408 | tf_op jit(solution)/shard_map/sections/pallas_call | solution.py:607
  72.6 2.7 %copy.21 = bf16[4,28,28,128]{3,0,2,1:T(4,128)(2,1)} copy(bf16[4,28,28,128]{3,2,1,0:T(8,128)(2,1)} %get-tuple-element.3) | data formatting | bytes 1605632 | tf_op jit(solution)/shard_map/sections/pallas_call | solution.py:607

commit v3 on v2

--- a/solution.py
+++ b/solution.py
@@ -77,6 +77,7 @@
     q_wide = jnp.concatenate([padded(q), padded((hot - 1.0) * chosen)], 1)
     k_wide = jnp.concatenate([jnp.concatenate([k * head_mask(head), hot], 1) for head in range(4)], 0)
     scores = dot_t(k_wide, q_wide)
+    yield
     out = []
     for head in range(4):
         rows = slice(ROWS * head, ROWS * head + ROWS)
@@ -86,6 +87,7 @@
             raised = jnp.exp2(part - jnp.max(part, 0, keepdims=True))
             share = 1.0 / jnp.sum(raised, 0, keepdims=True)
             probs_ref[at, rows, lanes] = (raised * share).astype(BF16)
+        yield
         out.append(dot(values_t[HEAD * head : HEAD * head + HEAD], probs_ref[at, rows, :]))
     return jnp.concatenate(out, 0)
 
@@ -94,6 +96,7 @@
     product = d_out_t * out_t
     values = jnp.concatenate([values * head_mask(head) for head in range(4)], 0)
     d_probs = dot_t(values, d_out)
+    yield
     d_queries = []
     d_scores = []
     for head in range(4):
@@ -101,13 +104,21 @@
         own = slice(HEAD * head, HEAD * head + HEAD)
         delta = jnp.sum(product[own], 0, keepdims=True)
         d_scores.append((probs_ref[at, rows, :].astype(F32) * (d_probs[rows] - delta)).astype(BF16))
+        yield
         d_queries.append(dot(keys_t[own], d_scores[head]))
     all_values = dot(probs_ref[at], d_out)
     all_keys = dot(jnp.concatenate(d_scores, 0), padded(q))
+    yield
     d_values = pick_heads(all_values)
     d_keys = pick_heads(all_keys) * LN2
     d_q = jnp.transpose(jnp.concatenate(d_queries, 0) * SCALE)[:ROWS]
     return jnp.concatenate([d_q.astype(BF16), d_keys.astype(BF16), d_values.astype(BF16)], 1)
+
+
+def together(parts):
+    parts = list(parts)
+    while parts:
+        parts = [part for part in parts if next(part, parts) is None]
 
 
 def pick_heads(stacked):
@@ -199,6 +210,8 @@
     section_out,
     grad_out,
     held,
+    cot_rows,
+    cot_stage,
     cot_held,
     hot,
     seam_out,
@@ -276,7 +289,7 @@
         return moved[-1]
 
     tokens_own = local(tokens.at[2:4, FIRST:28], held.at[0:2, 0:OWN])
-    cot_own = local(cotangent.at[2:4, 3:7], cot_held.at[0:2, 0:4])
+    cot_own = local(cot_stage.at[2:4, 3:7], cot_held.at[0:2, 0:4])
     weights = [
         local(projection_three_hbm, projection_three),
         local(merge_weight_one_hbm, merge_weight_one),
@@ -288,9 +301,9 @@
     tokens_ha = remote(tokens.at[2:4, 0:FIRST], held.at[0:2, OWN:28], behind[1])
     tokens_both = remote(tokens.at[0:2, 0:FIRST], held.at[2:4, OWN:28], behind[2])
     hot_ha = remote(hot.at[0], hot.at[1], behind[1])
-    cot_ta = remote(cotangent.at[0:2, 3:7], cot_held.at[2:4, 0:4], behind[0])
-    cot_ha = remote(cotangent.at[2:4, 0:3], cot_held.at[0:2, 4:7], behind[1])
-    cot_both = remote(cotangent.at[0:2, 0:3], cot_held.at[2:4, 4:7], behind[2])
+    cot_ta = remote(cot_stage.at[0:2, 3:7], cot_held.at[2:4, 0:4], behind[0])
+    cot_ha = remote(cot_stage.at[2:4, 0:3], cot_held.at[0:2, 4:7], behind[1])
+    cot_both = remote(cot_stage.at[0:2, 0:3], cot_held.at[2:4, 4:7], behind[2])
     seam = remote(seam_out, seam_in, behind[1])
     back = remote(back_out, back_in, ahead[1])
     section_copies = [
@@ -313,14 +326,22 @@
     for device in ahead + behind:
         pl.semaphore_signal(barrier, inc=1, device_id=device, device_id_type=pl.DeviceIdType.MESH)
     pl.semaphore_wait(barrier, 6)
-    for copy in (tokens_ta, tokens_both, tokens_ha, tokens_ta_rest, cot_ta, cot_both, cot_ha):
+    for copy in (tokens_ta, tokens_both, tokens_ha, tokens_ta_rest):
         copy.start()
     for copy in weights:
         copy.start()
-    cot_own.start()
 
     region_classes(regions_one, regions_three, hot)
     hot_ha.start()
+    for row in range(7):
+        source = cotangent[row].astype(F32)
+        for column in range(7):
+            for frame in range(4):
+                cot_rows[frame, row, column : column + 1, :] = source[column, frame : frame + 1, :]
+        for frame in range(4):
+            cot_stage[frame, row] = cot_rows[frame, row].astype(BF16)
+    for copy in (cot_ta, cot_both, cot_ha, cot_own):
+        copy.start()
     expand_tables(table_one, table_three, bias_one, bias_three, tables, wide)
     for part in range(2):
         weight = projection_one[:, C1 * (part + 1) : C1 * (part + 2)].astype(F32)
@@ -336,14 +357,16 @@
         x = windows[at]
         hat, _unused = normalised(x)
         normed = (hat * gain_one[...]).astype(BF16)
+        yield
         packed = dot(normed, projection_one[...])
         packed_t = dot_t(kv_one_t[...], normed).astype(BF16)
+        yield
         q = (packed[:, :C1] * (SCALE * LOG2E)).astype(BF16)
         v_one[at] = packed[:, 2 * C1 :].astype(BF16)
         q_one[at] = q
         kt_one[at] = packed_t[:C1]
         hot_at = 4 * (4 * lax.rem(k + 1, 4) + m)
-        out_t = attend(
+        out_t = yield from attend(
             q,
             packed[:, C1 : 2 * C1].astype(BF16),
             packed_t[C1:],
@@ -354,6 +377,7 @@
             probs_one,
             at,
         )
+        yield
         out_t_one[at] = out_t.astype(BF16)
         out = jnp.transpose(out_t)[:ROWS].astype(BF16)
         mixed[at] = rounded(x + rounded(dot(out, outward_one[...])))
@@ -385,11 +409,7 @@
                 for m in range(4):
                     windows[4 * k + m, group : group + 8, :] = grid[frame, row, 3 + 7 * m : 11 + 7 * m, :]
 
-        def one(m, _):
-            forward_one(k, m)
-            return 0
-
-        lax.fori_loop(0, 4, one, 0, unroll=4)
+        together(forward_one(k, m) for m in range(4))
 
         for frame in range(4):
             for row in range(7):
@@ -455,13 +475,12 @@
         kt_three[g] = packed_t[C1 * g : C1 * g + C1]
         vt_three[g] = packed_t[C3 + C1 * g : C3 + C1 * g + C1]
 
-    def forward_three(g, _):
-        out_t = attend(q_three[g], k_three[g], vt_three[g], hot[0], 64, bias_three, g, probs_three, g)
+    def forward_three(g):
+        out_t = yield from attend(q_three[g], k_three[g], vt_three[g], hot[0], 64, bias_three, g, probs_three, g)
         out_t_three[g] = out_t.astype(BF16)
         out_three[g] = jnp.transpose(out_t)[:ROWS].astype(BF16)
-        return 0
-
-    lax.fori_loop(0, 4, forward_three, 0, unroll=4)
+
+    together(forward_three(g) for g in range(4))
     out = jnp.concatenate([out_three[g] for g in range(4)], 1)
     cot_wide[...] = merged_two + rounded(dot(out, outward_three[...]))
     for frame in range(4):
@@ -490,8 +509,8 @@
         d_out_three[g] = d_out[:, C1 * g : C1 * g + C1]
         d_out_t_three[g] = d_out_t[C1 * g : C1 * g + C1]
 
-    def backward_three(g, _):
-        d_packed_three[g] = attend_pull(
+    def backward_three(g):
+        d_packed_three[g] = yield from attend_pull(
             d_out_three[g],
             d_out_t_three[g],
             out_t_three[g].astype(F32),
@@ -501,9 +520,8 @@
             probs_three,
             g,
         )
-        return 0
-
-    lax.fori_loop(0, 4, backward_three, 0, unroll=4)
+
+    together(backward_three(g) for g in range(4))
     d_packed = jnp.concatenate(
         [d_packed_three[g, :, C1 * part : C1 * part + C1] for part in range(3) for g in range(4)], 1
     )
@@ -540,7 +558,8 @@
         d_mixed = padded(d_residual.astype(BF16))
         d_out = dot_t(d_mixed, outward_one[...]).astype(BF16)
         d_out_t = dot_t(outward_one[...], d_mixed)
-        d_packed = attend_pull(
+        yield
+        d_packed = yield from attend_pull(
             d_out, d_out_t, out_t_one[at].astype(F32), q_one[at], kt_one[at], v_one[at], probs_one, at
         )
         d_normed = rounded(dot_t(d_packed, projection_one[...]))
@@ -564,11 +583,7 @@
                 for m in range(1, 4):
                     mixed[4 * k + m, group : group + 8, :] = folded[frame, 7 * k + row, 7 * m : 7 * m + 8, :]
 
-        def one(m, _):
-            backward_one(4 * k + m)
-            return 0
-
-        lax.fori_loop(0, 4, one, 0, unroll=4)
+        together(backward_one(4 * k + m) for m in range(4))
 
         for frame in range(4):
             for row in range(7):
@@ -603,7 +618,7 @@
 def main_call(mesh_shape, *operands):
     vmem = pl.BlockSpec(memory_space=pltpu.VMEM)
     hbm = pl.BlockSpec(memory_space=pl.ANY)
-    in_specs = [hbm, hbm, vmem, vmem, vmem, vmem, vmem, vmem, vmem, vmem, hbm, vmem, hbm, vmem, hbm, hbm]
+    in_specs = [hbm, vmem, vmem, vmem, vmem, vmem, vmem, vmem, vmem, vmem, hbm, vmem, hbm, vmem, hbm, hbm]
     return pl.pallas_call(
         functools.partial(main_kernel, *mesh_shape),
         out_shape=(
@@ -614,6 +629,8 @@
         out_specs=(hbm, hbm),
         scratch_shapes=[
             pltpu.VMEM((4, 28, 28, C1), BF16),
+            pltpu.VMEM((4, 7, 7, C3), F32),
+            pltpu.VMEM((4, 7, 7, C3), BF16),
             pltpu.VMEM((4, 7, 7, C3), BF16),
             pltpu.VMEM((2, ROWS, 128), BF16),
             pltpu.VMEM((4, 2, CELLS, C1), BF16),
@@ -689,7 +706,7 @@
     return main_call(
         (lax.axis_size("ha"), lax.axis_size("ta")),
         tokens,
-        cotangent,
+        cotangent.transpose(1, 2, 0, 3),
         regions_one.transpose(1, 0, 2),
         regions_three.transpose(1, 0, 2),
         table_one.T,

time: 75.6 us -> 67.5 us (0.89)
  Pallas kernels: 66.4 us -> 60 us
  local copies, waits for them, and re-layouts: 8.28 us -> 6.63 us
    pallas_call x1, Pallas kernels: 66.4 us -> 60 us  [main_call(): pl.pallas_call(functools.partial(main_kernel, *mesh_shape), out_shape=(ja...]
    unnamed x2 -> x1, local copies, waits for them, and re-layouts: 3.87 us -> 2.21 us
where the time goes in v3:
time: 67.5 us; the launch traced here: 67.2 us
  Pallas kernels  60 us (89%)
  local copies, waits for them, and re-layouts  6.63 us (10%)
    pallas_call x1, Pallas kernels, main_call(): pl.pallas_call(functools.partial(main_kernel, *mesh_shape), out_shape=(ja...  60 us
    pallas_call x2, local copies, waits for them, and re-layouts, main_call(): pl.pallas_call(functools.partial(main_kernel, *mesh_shape), out_shape=(ja...  4.41 us
    unnamed x1, local copies, waits for them, and re-layouts  2.21 us

profile of v3, /device:TPU:1, one launch (start us, length us, event | category | flops | bytes accessed | tf_op | source)
XLA Modules:
  0.0 67.2 jit_solution(11606543979056182583)
XLA Ops:
  0.6 2.2 %copy.18.tokens = bf16[4,28,28,128]{3,2,1,0:T(8,128)(2,1)} copy(bf16[4,28,28,128]{3,0,2,1:T(4,128)(2,1)} %param.16) | data formatting | bytes 1605632 | tf_op args[0]
  2.8 60.0 %sections.1 = (bf16[4,7,7,512]{3,2,1,0:T(8,128)(2,1)}, bf16[4,28,28,128]{3,2,1,0:T(8,128)(2,1)}) custom-call(bf16[4,28,28,128]{3,2,1,0:T(8,128)(2,1)} %copy.18.tokens, bf16[7,7,4,512]{3,2,1,0:T(4,128)(2,1)} %bitcast.9, s32[28,4,28]{2,1,0:T(4,128)} %bitcast.11, s32[7,4,7]{2,1,0:T(4,128)} %bitcast.13, f32[4,1183]{1,0:T(4,128)} %bitcast.12, ...), custom_call_target="tpu_custom_call" | custom-call | flops 30000001024 | bytes 20000000 | tf_op jit(solution)/shard_map/sections/pallas_call | solution.py:622
  62.8 1.7 %copy.19 = bf16[4,7,7,512]{3,0,2,1:T(4,128)(2,1)} copy(bf16[4,7,7,512]{3,2,1,0:T(8,128)(2,1)} %get-tuple-element.2) | data formatting | bytes 401408 | tf_op jit(solution)/shard_map/sections/pallas_call | solution.py:622
  64.6 2.7 %copy.20 = bf16[4,28,28,128]{3,0,2,1:T(4,128)(2,1)} copy(bf16[4,28,28,128]{3,2,1,0:T(8,128)(2,1)} %get-tuple-element.3) | data formatting | bytes 1605632 | tf_op jit(solution)/shard_map/sections/pallas_call | solution.py:622

commit v4 on v3

--- a/solution.py
+++ b/solution.py
@@ -326,13 +326,12 @@
     for device in ahead + behind:
         pl.semaphore_signal(barrier, inc=1, device_id=device, device_id_type=pl.DeviceIdType.MESH)
     pl.semaphore_wait(barrier, 6)
-    for copy in (tokens_ta, tokens_both, tokens_ha, tokens_ta_rest):
+    for copy in (tokens_ta, tokens_ha):
         copy.start()
     for copy in weights:
         copy.start()
 
     region_classes(regions_one, regions_three, hot)
-    hot_ha.start()
     for row in range(7):
         source = cotangent[row].astype(F32)
         for column in range(7):
@@ -340,9 +339,11 @@
                 cot_rows[frame, row, column : column + 1, :] = source[column, frame : frame + 1, :]
         for frame in range(4):
             cot_stage[frame, row] = cot_rows[frame, row].astype(BF16)
-    for copy in (cot_ta, cot_both, cot_ha, cot_own):
+    tokens_ta_rest.start()
+    cot_own.start()
+    expand_tables(table_one, table_three, bias_one, bias_three, tables, wide)
+    for copy in (tokens_both, hot_ha, cot_ta, cot_ha, cot_both):
         copy.start()
-    expand_tables(table_one, table_three, bias_one, bias_three, tables, wide)
     for part in range(2):
         weight = projection_one[:, C1 * (part + 1) : C1 * (part + 2)].astype(F32)
         kv_one_t[C1 * part : C1 * part + C1, :] = jnp.transpose(weight).astype(BF16)

time: 67.5 us -> 68.3 us (1.012)
  Pallas kernels: 60 us -> 60.8 us
    pallas_call x1, Pallas kernels: 60 us -> 60.8 us  [main_call(): pl.pallas_call(functools.partial(main_kernel, *mesh_shape), out_shape=(ja...]
where the time goes in v4:
time: 68.3 us; the launch traced here: 68.1 us
  Pallas kernels  60.8 us (89%)
  local copies, waits for them, and re-layouts  6.63 us (10%)
    pallas_call x1, Pallas kernels, main_call(): pl.pallas_call(functools.partial(main_kernel, *mesh_shape), out_shape=(ja...  60.8 us
    pallas_call x2, local copies, waits for them, and re-layouts, main_call(): pl.pallas_call(functools.partial(main_kernel, *mesh_shape), out_shape=(ja...  4.41 us
    unnamed x1, local copies, waits for them, and re-layouts  2.21 us

profile of v4, /device:TPU:1, one launch (start us, length us, event | category | flops | bytes accessed | tf_op | source)
XLA Modules:
  0.0 68.1 jit_solution(10475985034117256875)
XLA Ops:
  0.6 2.2 %copy.18.tokens = bf16[4,28,28,128]{3,2,1,0:T(8,128)(2,1)} copy(bf16[4,28,28,128]{3,0,2,1:T(4,128)(2,1)} %param.16) | data formatting | bytes 1605632 | tf_op args[0]
  2.8 60.8 %sections.1 = (bf16[4,7,7,512]{3,2,1,0:T(8,128)(2,1)}, bf16[4,28,28,128]{3,2,1,0:T(8,128)(2,1)}) custom-call(bf16[4,28,28,128]{3,2,1,0:T(8,128)(2,1)} %copy.18.tokens, bf16[7,7,4,512]{3,2,1,0:T(4,128)(2,1)} %bitcast.9, s32[28,4,28]{2,1,0:T(4,128)} %bitcast.11, s32[7,4,7]{2,1,0:T(4,128)} %bitcast.13, f32[4,1183]{1,0:T(4,128)} %bitcast.12, ...), custom_call_target="tpu_custom_call" | custom-call | flops 30000001024 | bytes 20000000 | tf_op jit(solution)/shard_map/sections/pallas_call | solution.py:623
  63.6 1.7 %copy.19 = bf16[4,7,7,512]{3,0,2,1:T(4,128)(2,1)} copy(bf16[4,7,7,512]{3,2,1,0:T(8,128)(2,1)} %get-tuple-element.2) | data formatting | bytes 401408 | tf_op jit(solution)/shard_map/sections/pallas_call | solution.py:623
  65.4 2.7 %copy.20 = bf16[4,28,28,128]{3,0,2,1:T(4,128)(2,1)} copy(bf16[4,28,28,128]{3,2,1,0:T(8,128)(2,1)} %get-tuple-element.3) | data formatting | bytes 1605632 | tf_op jit(solution)/shard_map/sections/pallas_call | solution.py:623
